TPU v7x, 512 devices: a whole 4x8x8 slice. The times are simulated.
512 devices in a mesh: grid: 128 (over x, z, y_hi, core), state: 4 (over y_lo).
Axes of the slice: x: 4, y: 8 (y_hi: 2, y_lo: 4; y = y_hi * 4 + y_lo), z: 8, core: 2. Of those that a mesh axis runs over, the one named last changes fastest.
Arguments:
- x_block: float32 [262144, 512], P('grid', 'state'), as said below
- h_block: float32 [262144, 512], P('grid', 'state'), as said below
- mass_weights: float32 [262144], P('grid'), as said below
- coefficients: float32 [512, 512], P(None, 'state'), may hold values from -0.25 to 0.25
Outputs:
- rotated: float32 [262144, 512], P('grid', 'state')
- projected: float32 [512, 512], P(None, 'state')
Inputs may be any that keep to these rules, and one draw needn't show every extreme that they name: x_block is a real field whose columns are correlated with their neighbours so that gram is positive definite. h_block's values are of the magnitude of x_block's. `mass_weights`: positive weights of order 1 / 262144.
All inputs are finite; a program needn't handle non-finite values.
Results may differ from a plain program's by a relative error of at most 0.00024.
Values sent between devices are 32-bit elements; how exact they have to be, the bound alone decides.
No kernel may reach another device: no remote copies, remote signals or barrier semaphores. Data moves between devices by JAX's collectives and lax.ppermute only.
A program may use at most 64 MiB of HBM per device.

v0:
```python
import functools

import jax
import jax.numpy as jnp
from jax import lax
from jax.experimental import pallas as pl
from jax.experimental.pallas import tpu as pltpu
from jax.sharding import Mesh, PartitionSpec as P

GRID = ("x", "z", "yh", "core")
ALL = GRID + ("state",)
PLANE = ("x", "z")
LINE = ("yh", "state")
HIGHEST = lax.Precision.HIGHEST
EDGE, SUB = 128, 8
dot = functools.partial(lax.dot_general, precision=HIGHEST, preferred_element_type=jnp.float32)
PLAIN, BY_ROWS, BY_COLS = (((1,), (0,)), ((), ())), (((1,), (1,)), ((), ())), (((0,), (0,)), ((), ()))


def after(value, *earlier):
    return lax.optimization_barrier((value, *earlier))[0]


def exchange(value, axes):
    return lax.all_to_all(value, axes, 0, 0, tiled=True)


def total(value, axes):
    return jnp.sum(value.reshape(lax.axis_size(axes), -1, value.shape[1]), axis=0)


def copies(value, axes):
    count = lax.axis_size(axes)
    return jnp.broadcast_to(value, (count,) + value.shape).reshape(-1, value.shape[1])


def block_inverse(rows):
    at_row = lax.broadcasted_iota(jnp.int32, (SUB, EDGE), 0)
    at_lane = lax.broadcasted_iota(jnp.int32, (SUB, EDGE), 1)
    groups = len(rows)
    left = list(rows)
    right = [jnp.where(at_lane == at_row + SUB * g, 1.0, 0.0).astype(jnp.float32) for g in range(groups)]

    def spread_row(value, c):
        return jnp.broadcast_to(value[c : c + 1, :], (SUB, EDGE))

    def spread_col(value, c):
        return jnp.broadcast_to(value[:, c : c + 1], (SUB, EDGE))

    for k in range(groups):
        cols = {g: [spread_col(left[g], SUB * k + c) for c in range(SUB)] for g in range(k, groups)}
        for c in range(SUB):
            scale = lax.rsqrt(spread_row(cols[k][c], c))
            inv = scale * scale
            left_row, right_row = spread_row(left[k], c), spread_row(right[k], c)
            col_row = {d: spread_row(cols[k][d], c) for d in range(c + 1, SUB)}
            below = jnp.where(at_row > c, cols[k][c], 0.0)
            for d in range(c + 1, SUB):
                cols[k][d] = cols[k][d] - (below * col_row[d]) * inv
            left[k] = left[k] - (below * left_row) * inv
            right[k] = jnp.where(at_row == c, right_row * scale, right[k] - (below * right_row) * inv)
            for g in range(k + 1, groups):
                factor = cols[g][c] * inv
                for d in range(c + 1, SUB):
                    cols[g][d] = cols[g][d] - factor * col_row[d]
                left[g] = left[g] - factor * left_row
                right[g] = right[g] - factor * right_row
    return right


def pack(matrix, first_rows):
    return jnp.concatenate(
        [matrix[first:, EDGE * j : EDGE * (j + 1)] for j, first in enumerate(first_rows)], axis=0
    )


def panel_pieces(first_rows, nb, splits):
    pieces, at = [], 0
    for first in first_rows:
        panel, row, end = [], first, at + nb - first
        while at < end:
            (low, high, offset) = next(s for s in splits if s[0] <= at < s[1])
            count = min(end, high) - at
            panel.append((row, count, at - low + offset))
            row, at = row + count, at + count
        pieces.append(panel)
    return pieces


def small_matrices(gram_pieces, hamil_pieces, state_ref, packed, coefficients, rotation_ref, projected_ref, work, inverse, block):
    nb = work.shape[0]
    blocks = nb // EDGE
    work[...] = jnp.zeros((nb, nb), jnp.float32)
    inverse[...] = jnp.zeros((nb, nb), jnp.float32)
    for j, panel in enumerate(gram_pieces):
        for row, count, at in panel:
            work[row : row + count, EDGE * j : EDGE * (j + 1)] = packed[at : at + count, :]

    @pl.loop(0, blocks)
    def _(k):
        start = pl.multiple_of(k * EDGE, EDGE)
        rows = [
            work[pl.ds(pl.multiple_of(start + SUB * g, SUB), SUB), pl.ds(start, EDGE)]
            for g in range(EDGE // SUB)
        ]
        for g, row in enumerate(block_inverse(rows)):
            block[SUB * g : SUB * (g + 1), :] = row

        for j in range(blocks):

            @pl.when(k == j)
            def _():
                low, high = EDGE * j, EDGE * (j + 1)
                inverse[low:high, low:high] = block[...]
                if j + 1 < blocks:
                    panel = dot(work[high:, low:high], block[...], BY_ROWS)
                    work[high:, high:] = work[high:, high:] - dot(panel, panel, BY_ROWS)
                if j:
                    inverse[low:high, :low] = dot(block[...], inverse[low:high, :low], PLAIN)
                if j + 1 < blocks:
                    inverse[high:, :high] = inverse[high:, :high] - dot(panel, inverse[low:high, :high], PLAIN)

    for j in range(blocks):
        low, high = EDGE * j, EDGE * (j + 1)
        rotation_ref[low:high, :] = dot(inverse[low:, low:high], coefficients[low:, :], BY_COLS)
    own = pl.ds(pl.multiple_of(state_ref[0] * EDGE, EDGE), EDGE)
    half = jnp.zeros((nb, EDGE), jnp.float32)
    for j, panel in enumerate(hamil_pieces):
        columns = jnp.concatenate([packed[at : at + count, :] for _, count, at in panel], axis=0)
        half = half + dot(columns, inverse[own, EDGE * j : EDGE * (j + 1)], BY_ROWS)
    for j in range(blocks):
        high = EDGE * (j + 1)
        projected_ref[high - EDGE : high, :] = dot(inverse[high - EDGE : high, :high], half[:high], PLAIN)


def solve(state, packed, coefficients, gram_pieces, hamil_pieces):
    nb = coefficients.shape[0]
    in_vmem = pl.BlockSpec(memory_space=pltpu.VMEM)
    result = jax.ShapeDtypeStruct(coefficients.shape, jnp.float32)
    square = pltpu.VMEM((nb, nb), jnp.float32)
    return pl.pallas_call(
        functools.partial(small_matrices, gram_pieces, hamil_pieces),
        out_shape=(result, result),
        in_specs=[pl.BlockSpec(memory_space=pltpu.SMEM), in_vmem, in_vmem],
        out_specs=(in_vmem, in_vmem),
        scratch_shapes=[square, square, pltpu.VMEM((EDGE, EDGE), jnp.float32)],
        cost_estimate=pl.CostEstimate(flops=2 * 10**10, bytes_accessed=2**22, transcendentals=0),
        compiler_params=pltpu.CompilerParams(vmem_limit_bytes=32 * 2**20),
    )(state, packed, coefficients)


def other_core(value):
    core, count = lax.axis_index("core"), value.shape[0] // 2
    kept = lax.dynamic_slice_in_dim(value, core * count, count, 0)
    sent = lax.dynamic_slice_in_dim(value, (1 - core) * count, count, 0)
    return kept + lax.ppermute(sent, "core", [(0, 1), (1, 0)])


def shards(x_block, h_block, mass_weights, coefficients):
    state = lax.axis_index("state")
    x_rows = lax.all_to_all(x_block, "state", 0, 1, tiled=True)
    points, nb = x_rows.shape
    h_rows = lax.all_to_all(after(h_block, x_rows), "state", 0, 1, tiled=True)
    gathered = lax.all_gather(after(x_block, h_rows), "state", axis=1, tiled=True)
    weights = lax.dynamic_slice_in_dim(mass_weights, state * points, points, 0)
    weighted_x = weights[:, None] * x_rows

    gram_firsts = [0 if EDGE * j < nb // 2 else nb // 2 for j in range(nb // EDGE)]
    hamil_firsts = [0] * (nb // EDGE)
    gram = other_core(pack(dot(x_rows, weighted_x, BY_COLS), gram_firsts))
    hamil = other_core(pack(dot(weighted_x, h_rows, BY_COLS), hamil_firsts))
    gram_rows, hamil_rows = gram.shape[0], hamil.shape[0]
    both = jnp.concatenate([gram, hamil], axis=0)
    both_rows = gram_rows + hamil_rows
    both = total(exchange(both, PLANE), PLANE)
    both = total(exchange(copies(both, LINE), LINE), LINE)
    both = exchange(copies(both, PLANE), PLANE)
    both = exchange(copies(both, "core"), "core")
    gram_splits = [(0, gram_rows, 0), (gram_rows, 2 * gram_rows, both_rows)]
    hamil_splits = [(0, hamil_rows, gram_rows), (hamil_rows, 2 * hamil_rows, both_rows + gram_rows)]
    rotation, projected = solve(
        state[None],
        both,
        coefficients,
        panel_pieces(gram_firsts, nb, gram_splits),
        panel_pieces(hamil_firsts, nb, hamil_splits),
    )
    rotated = jnp.dot(gathered, rotation, precision=lax.Precision.HIGH)
    return (rotated, projected)


def solution(mesh):
    split = Mesh(mesh.devices.reshape(4, 8, 2, 2, 4), ALL)
    placed = (P(GRID, "state"), P(GRID, "state"), P(GRID), P(None, "state"))
    return jax.shard_map(
        shards,
        mesh=split,
        in_specs=placed,
        out_specs=(P(GRID, "state"), P(None, "state")),
        check_vma=False,
    )
```

profile of v0, /device:TPU:1, one launch (start us, length us, event | category | flops | bytes accessed | tf_op | source)
XLA Modules:
  0.0 210.4 jit_solution(14688084666450711030)
XLA Ops:
  7.2 29.3 %all_to_all.70 = f32[4,512,128]{2,1,0:T(8,128)S(1)} all-to-all(f32[4,512,128]{2,1,0:T(8,128)} %bitcast.26), channel_id=1, replica_groups=mesh['x'=4,'z'=8,'yh'=2,'core'=2,'state'=4] {'state'}, dimensions={0} | all-to-all | bytes 2097152 | tf_op jit(solution)/shard_map/all_to_all | solution.py:161
  36.5 0.3 copy.9
  36.8 4.3 %all-to-all-start.1 = ((f32[4,512,128]{2,1,0:T(8,128)}), f32[4,512,128]{2,1,0:T(8,128)}, u32[]{:S(2)}, u32[]{:S(2)}) async-start(f32[4,512,128]{2,1,0:T(8,128)} %bitcast.3), calls=%async_computation.1 | async-start | bytes 2097152 | tf_op jit(solution)/shard_map/all_to_all | solution.py:163
  41.1 0.0 all-gather.2.cloned.1.call-start
  41.1 0.8 dynamic_slice.15
  41.9 0.1 broadcast_multiply_fusion
  42.0 0.3 copy.11
  42.4 1.9 convolution_bitcast_fusion
  44.3 0.1 pad_maximum_fusion.2
  44.4 0.8 constant_dynamic-slice_fusion.1
  45.2 4.7 %collective-permute-start = (f32[768,128]{1,0:T(8,128)}, f32[768,128]{1,0:T(8,128)}, u32[]{:S(2)}, u32[]{:S(2)}) collective-permute-start(f32[768,128]{1,0:T(8,128)} %constant_dynamic-slice_fusion.1), channel_id=1, source_target_pairs={{0,4},{4,0},{1,5},{5,1},{2,6},{6,2},{3,7},{7,3},{8,12},{12,8},{9,1... | collective-permute-start | bytes 1179656 | tf_op jit(solution)/shard_map/ppermute | solution.py:156
  49.9 16.5 %all-to-all-done.1 = f32[4,512,128]{2,1,0:T(8,128)} async-done(((f32[4,512,128]{2,1,0:T(8,128)}), f32[4,512,128]{2,1,0:T(8,128)}, u32[]{:S(2)}, u32[]{:S(2)}) %all-to-all-start.1) | async-done | bytes 1048608 | tf_op jit(solution)/shard_map/all_to_all | solution.py:163
  66.3 1.6 copy.10
  67.9 1.9 fusion.3
  69.8 0.1 fusion.2
  69.8 0.1 pad_maximum_fusion
  70.0 3.4 %collective-permute-start.1 = (f32[1024,128]{1,0:T(8,128)S(1)}, f32[1024,128]{1,0:T(8,128)S(1)}, u32[]{:S(2)}, u32[]{:S(2)}) collective-permute-start(f32[1024,128]{1,0:T(8,128)S(1)} %constant_dynamic-slice_fusion), channel_id=1, source_target_pairs={{0,4},{4,0},{1,5},{5,1},{2,6},{6,2},{3,7},{7,3},{8,12},{12,8},{9,1... | collective-permute-start | bytes 1572872 | tf_op jit(solution)/shard_map/ppermute | solution.py:156
  73.4 0.0 collective-permute-done
  73.4 1.0 dynamic-slice_add_fusion.1
  74.4 0.0 all-gather.2.cloned.1.call-update
  74.4 0.4 collective-permute-done.1
  74.9 0.1 dynamic-slice_add_fusion
  74.9 0.1 pad_maximum_fusion.1
  75.0 36.0 %all_to_all.71 = f32[32,56,128]{2,1,0:T(8,128)S(1)} all-to-all(f32[32,56,128]{2,1,0:T(8,128)S(1)} %bitcast.27), channel_id=1, replica_groups=mesh['x'=4,'z'=8,'yh'=2,'core'=2,'state'=4] {'x','z'}, dimensions={0} | all-to-all | bytes 1835008 | tf_op jit(solution)/shard_map/all_to_all | solution.py:25
  111.0 0.1 reduce_sum.18
  111.1 17.1 %all_to_all.72 = f32[8,56,128]{2,1,0:T(8,128)S(1)} all-to-all(f32[8,56,128]{2,1,0:T(8,128)S(1)} %broadcast_in_dim.14), channel_id=1, replica_groups=mesh['x'=4,'z'=8,'yh'=2,'core'=2,'state'=4] {'yh','state'}, dimensions={0} | all-to-all | bytes 458752 | tf_op jit(solution)/shard_map/all_to_all | solution.py:25
  128.2 0.1 broadcast_in_dim.15
  128.2 0.0 copy-start
  128.3 34.1 %all_to_all.73 = f32[32,56,128]{2,1,0:T(8,128)S(1)} all-to-all(f32[32,56,128]{2,1,0:T(8,128)S(1)} %broadcast_in_dim.15), channel_id=1, replica_groups=mesh['x'=4,'z'=8,'yh'=2,'core'=2,'state'=4] {'x','z'}, dimensions={0} | all-to-all | bytes 1835008 | tf_op jit(solution)/shard_map/all_to_all | solution.py:25
  162.3 0.1 broadcast_in_dim.16
  162.5 12.5 %all_to_all.74 = f32[2,1792,128]{2,1,0:T(8,128)S(1)} all-to-all(f32[2,1792,128]{2,1,0:T(8,128)S(1)} %broadcast_in_dim.16), channel_id=1, replica_groups=mesh['x'=4,'z'=8,'yh'=2,'core'=2,'state'=4] {'core'}, dimensions={0} | all-to-all | bytes 3670016 | tf_op jit(solution)/shard_map/all_to_all | solution.py:25
  175.0 0.0 copy-done
  175.0 23.6 %shard_map.59 = (f32[512,128]{1,0:T(8,128)S(1)}, f32[512,128]{1,0:T(8,128)}) custom-call(s32[1]{0:T(128)} %bitcast.6.state_ref, f32[3584,128]{1,0:T(8,128)S(1)} %bitcast.20, f32[512,128]{1,0:T(8,128)S(1)} %copy-done), custom_call_target="tpu_custom_call" | custom-call | flops 20000000000 | bytes 4194304 | tf_op jit(solution)/shard_map/pallas_call | solution.py:141
  198.6 0.0 all-gather.2.cloned.1.call-done
  198.6 5.0 %fusion.4 = f32[2048,128]{1,0:T(8,128)} fusion(f32[2048,512]{1,0:T(8,128)} %all-gather.2.cloned.1.call-done, f32[512,128]{1,0:T(8,128)S(1)} %get-tuple-element.8), kind=kOutput, calls=%fused_computation.13 | convolution fusion | flops 805306368 | bytes 5505024 | tf_op jit(solution)/shard_map/dot_general | solution.py:188
  (5 shorter events, 0.1 us)
Async XLA Ops:
  36.8 29.5 %all-to-all-start.1 = ((f32[4,512,128]{2,1,0:T(8,128)}), f32[4,512,128]{2,1,0:T(8,128)}, u32[]{:S(2)}, u32[]{:S(2)}) async-start(f32[4,512,128]{2,1,0:T(8,128)} %bitcast.3), calls=%async_computation.1 | async-start | bytes 2097152 | tf_op jit(solution)/shard_map/all_to_all | solution.py:163
  41.1 157.6 %all-gather.2.cloned.1.call-start = ((), (), s32[]{:S(2)}) async-start(), calls=%async_computation.6 | async-start | bytes 5242880 | tf_op jit(solution)/shard_map/all_gather | solution.py:164
  45.2 28.2 %collective-permute-start = (f32[768,128]{1,0:T(8,128)}, f32[768,128]{1,0:T(8,128)}, u32[]{:S(2)}, u32[]{:S(2)}) collective-permute-start(f32[768,128]{1,0:T(8,128)} %constant_dynamic-slice_fusion.1), channel_id=1, source_target_pairs={{0,4},{4,0},{1,5},{5,1},{2,6},{6,2},{3,7},{7,3},{8,12},{12,8},{9,1... | collective-permute-start | bytes 1179656 | tf_op jit(solution)/shard_map/ppermute | solution.py:156
  70.0 4.9 %collective-permute-start.1 = (f32[1024,128]{1,0:T(8,128)S(1)}, f32[1024,128]{1,0:T(8,128)S(1)}, u32[]{:S(2)}, u32[]{:S(2)}) collective-permute-start(f32[1024,128]{1,0:T(8,128)S(1)} %constant_dynamic-slice_fusion), channel_id=1, source_target_pairs={{0,4},{4,0},{1,5},{5,1},{2,6},{6,2},{3,7},{7,3},{8,12},{12,8},{9,1... | collective-permute-start | bytes 1572872 | tf_op jit(solution)/shard_map/ppermute | solution.py:156
  128.2 46.8 %copy-start = (f32[512,128]{1,0:T(8,128)S(1)}, f32[512,128]{1,0:T(8,128)}, u32[]{:S(2)}) copy-start(f32[512,128]{1,0:T(8,128)} %coefficients.1) | copy-start | bytes 786436
Sparse Core Ops, SparseCore 0:
  74.6 97.4 all-gather.1
where the time goes:
time: 213 us; the launch traced here: 210 us
  blocking collectives  129 us (61%)
  Pallas kernels  23.6 us (11%)
  waiting for transfers between devices  16.9 us (8%)
  between operations  14.2 us (7%)
  starting transfers between devices  12.4 us (6%)
  matrix products  8.68 us (4%)
  local copies, waits for them, and re-layouts  4.13 us (2%)
    all_to_all x4, blocking collectives, exchange(): return lax.all_to_all(value, axes, 0, 0, tiled=True)  99.7 us
    all_to_all x1, blocking collectives, shards(): x_rows = lax.all_to_all(x_block, 'state', 0, 1, tiled=True)  29.3 us
    pallas_call x1, Pallas kernels, solve(): pl.pallas_call(functools.partial(small_matrices, gram_pieces, hamil_piece...  23.6 us
    all_to_all x1, waiting for transfers between devices, shards(): h_rows = lax.all_to_all(after(h_block, x_rows), 'state', 0, 1, tiled=True)  16.5 us
    ppermute x2, starting transfers between devices, other_core(): return kept + lax.ppermute(sent, 'core', [(0, 1), (1, 0)])  8.08 us
    dot_general x1, matrix products, shards(): rotated = jnp.dot(gathered, rotation, precision=lax.Precision.HIGH)  4.96 us
  transfers between devices with their start and end apart: 4, of which 2 were waited for; matrix products, arithmetic and copies ran while one was open for 4% of the time, Pallas kernels for 11%

commit v1 on v0

v1 whole, which is shorter than its diff:
```python
import functools

import jax
import jax.numpy as jnp
from jax import lax
from jax.experimental import pallas as pl
from jax.experimental.pallas import tpu as pltpu
from jax.sharding import Mesh, PartitionSpec as P

GRID = ("x", "z", "yh", "core")
ALL = GRID + ("state",)
PLANE = ("x", "z")
LINE = ("yh", "state")
HIGHEST = lax.Precision.HIGHEST
EDGE, SUB, RUN = 128, 8, 16
dot = functools.partial(lax.dot_general, precision=HIGHEST, preferred_element_type=jnp.float32)
PLAIN, BY_ROWS, BY_COLS = (((1,), (0,)), ((), ())), (((1,), (1,)), ((), ())), (((0,), (0,)), ((), ()))


def after(value, *earlier):
    return lax.optimization_barrier((value, *earlier))[0]


def exchange(value, axes):
    return lax.all_to_all(value, axes, 0, 0, tiled=True)


def total(value, axes):
    return jnp.sum(value.reshape(lax.axis_size(axes), -1, value.shape[1]), axis=0)


def copies(value, axes):
    count = lax.axis_size(axes)
    return jnp.broadcast_to(value, (count,) + value.shape).reshape(-1, value.shape[1])


def block_inverse(rows):
    at_row = lax.broadcasted_iota(jnp.int32, (SUB, EDGE), 0)
    at_lane = lax.broadcasted_iota(jnp.int32, (SUB, EDGE), 1)
    groups = len(rows)
    left = list(rows)
    right = [jnp.where(at_lane == at_row + SUB * g, 1.0, 0.0).astype(jnp.float32) for g in range(groups)]

    def spread_row(value, c):
        return jnp.broadcast_to(value[c : c + 1, :], (SUB, EDGE))

    def spread_col(value, c):
        return jnp.broadcast_to(value[:, c : c + 1], (SUB, EDGE))

    for k in range(groups):
        cols = {g: [spread_col(left[g], SUB * k + c) for c in range(SUB)] for g in range(k, groups)}
        for c in range(SUB):
            scale = lax.rsqrt(spread_row(cols[k][c], c))
            inv = scale * scale
            left_row, right_row = spread_row(left[k], c), spread_row(right[k], c)
            col_row = {d: spread_row(cols[k][d], c) for d in range(c + 1, SUB)}
            below = jnp.where(at_row > c, cols[k][c], 0.0)
            for d in range(c + 1, SUB):
                cols[k][d] = cols[k][d] - (below * col_row[d]) * inv
            left[k] = left[k] - (below * left_row) * inv
            right[k] = jnp.where(at_row == c, right_row * scale, right[k] - (below * right_row) * inv)
            for g in range(k + 1, groups):
                factor = cols[g][c] * inv
                for d in range(c + 1, SUB):
                    cols[g][d] = cols[g][d] - factor * col_row[d]
                left[g] = left[g] - factor * left_row
                right[g] = right[g] - factor * right_row
    return right


def unpack(packed, states, matrix):
    nb = matrix.shape[0]
    for first in range(0, nb, RUN):
        for t in range(states):
            at = first * states + t * RUN
            matrix[first : first + RUN, EDGE * t : EDGE * (t + 1)] = packed[at : at + RUN, :]


def small_matrices(place_ref, own_packed, other_packed, coefficients, rotation_ref, projected_ref, work, hamil, inverse, block):
    nb = work.shape[0]
    blocks = nb // EDGE
    inverse[...] = jnp.zeros((nb, nb), jnp.float32)

    @pl.when(place_ref[0] == 0)
    def _():
        unpack(own_packed, blocks, work)
        unpack(other_packed, blocks, hamil)

    @pl.when(place_ref[0] != 0)
    def _():
        unpack(other_packed, blocks, work)
        unpack(own_packed, blocks, hamil)

    @pl.loop(0, blocks)
    def _(k):
        start = pl.multiple_of(k * EDGE, EDGE)
        rows = [
            work[pl.ds(pl.multiple_of(start + SUB * g, SUB), SUB), pl.ds(start, EDGE)]
            for g in range(EDGE // SUB)
        ]
        for g, row in enumerate(block_inverse(rows)):
            block[SUB * g : SUB * (g + 1), :] = row

        for j in range(blocks):

            @pl.when(k == j)
            def _():
                low, high = EDGE * j, EDGE * (j + 1)
                inverse[low:high, low:high] = block[...]
                if j + 1 < blocks:
                    panel = dot(work[high:, low:high], block[...], BY_ROWS)
                    work[high:, high:] = work[high:, high:] - dot(panel, panel, BY_ROWS)
                if j:
                    inverse[low:high, :low] = dot(block[...], inverse[low:high, :low], PLAIN)
                if j + 1 < blocks:
                    inverse[high:, :high] = inverse[high:, :high] - dot(panel, inverse[low:high, :high], PLAIN)

    for j in range(blocks):
        low, high = EDGE * j, EDGE * (j + 1)
        rotation_ref[low:high, :] = dot(inverse[low:, low:high], coefficients[low:, :], BY_COLS)
    own = pl.ds(pl.multiple_of(place_ref[1] * EDGE, EDGE), EDGE)
    half = dot(hamil[...], inverse[own, :], BY_ROWS)
    for j in range(blocks):
        high = EDGE * (j + 1)
        projected_ref[high - EDGE : high, :] = dot(inverse[high - EDGE : high, :high], half[:high], PLAIN)


def solve(place, own_packed, other_packed, coefficients):
    nb = coefficients.shape[0]
    in_vmem = pl.BlockSpec(memory_space=pltpu.VMEM)
    result = jax.ShapeDtypeStruct(coefficients.shape, jnp.float32)
    square = pltpu.VMEM((nb, nb), jnp.float32)
    return pl.pallas_call(
        small_matrices,
        out_shape=(result, result),
        in_specs=[pl.BlockSpec(memory_space=pltpu.SMEM), in_vmem, in_vmem, in_vmem],
        out_specs=(in_vmem, in_vmem),
        scratch_shapes=[square, square, square, pltpu.VMEM((EDGE, EDGE), jnp.float32)],
        cost_estimate=pl.CostEstimate(flops=2 * 10**10, bytes_accessed=2**22, transcendentals=0),
        compiler_params=pltpu.CompilerParams(vmem_limit_bytes=32 * 2**20),
    )(place, own_packed, other_packed, coefficients)


def high_low(value):
    high = value.astype(jnp.bfloat16)
    return high, (value - high.astype(jnp.float32)).astype(jnp.bfloat16)


def rotate_rows(source_ref, rotation_ref, *refs):
    *block_refs, rotated_ref = refs
    rows = [
        rotation_ref[pl.ds(pl.multiple_of(source_ref[b] * EDGE, EDGE), EDGE), :] for b in range(len(block_refs))
    ]
    turn_high, turn_low = high_low(jnp.concatenate(rows, axis=0))
    high, low = high_low(jnp.concatenate([ref[...] for ref in block_refs], axis=1))
    wide = jnp.dot(high, jnp.concatenate([turn_high, turn_low], axis=1), preferred_element_type=jnp.float32)
    small = wide[:, EDGE:] + jnp.dot(low, turn_high, preferred_element_type=jnp.float32)
    rotated_ref[...] = wide[:, :EDGE] + small


def rotate(sources, rotation, *blocks):
    rows, width = blocks[0].shape
    tile = rows // 4
    by_rows = pl.BlockSpec((tile, width), lambda i: (i, 0))
    return pl.pallas_call(
        rotate_rows,
        grid=(rows // tile,),
        out_shape=jax.ShapeDtypeStruct((rows, width), jnp.float32),
        in_specs=[
            pl.BlockSpec(memory_space=pltpu.SMEM),
            pl.BlockSpec(rotation.shape, lambda i: (0, 0)),
            *[by_rows] * len(blocks),
        ],
        out_specs=by_rows,
        cost_estimate=pl.CostEstimate(flops=2 * 10**9, bytes_accessed=6 * 2**20, transcendentals=0),
        compiler_params=pltpu.CompilerParams(vmem_limit_bytes=32 * 2**20),
    )(sources, rotation, *blocks)


def line_blocks(x_block, state):
    pairs = lax.ppermute(x_block, "state", [(0, 1), (1, 0), (2, 3), (3, 2)])
    middle = lax.ppermute(x_block, "state", [(1, 2), (2, 1)])
    outward = lax.ppermute(middle, "state", [(1, 0), (2, 3)])
    across = lax.ppermute(pairs, "state", [(1, 2), (2, 1)])
    far = lax.ppermute(across, "state", [(1, 0), (2, 3)])
    at_end = (state == 0) | (state == 3)
    return (
        (x_block, state),
        (pairs, state + 1 - 2 * (state % 2)),
        (jnp.where(at_end, outward, middle), jnp.where(state < 2, 2, 1)),
        (jnp.where(at_end, far, across), jnp.where(state < 2, 3, 0)),
    )


def shards(x_block, h_block, mass_weights, coefficients):
    state, core = lax.axis_index("state"), lax.axis_index("core")
    width = x_block.shape[1]
    blocks = line_blocks(x_block, state)
    weighted = mass_weights[:, None] * jnp.concatenate([x_block, h_block], axis=1)

    parts = jnp.zeros((2, len(blocks), width, width), jnp.float32)
    for block, source in blocks:
        product = dot(block, weighted, BY_COLS)
        product = jnp.stack([product[:, :width], product[:, width:]])
        parts = lax.dynamic_update_slice_in_dim(parts, product[:, None], source, 1)
    parts = parts.reshape(2, -1, width)

    kept = lax.dynamic_index_in_dim(parts, core, 0, keepdims=False)
    sent = lax.dynamic_index_in_dim(parts, 1 - core, 0, keepdims=False)
    summed = kept + lax.ppermute(sent, "core", [(0, 1), (1, 0)])
    summed = total(exchange(summed, PLANE), PLANE)
    summed = total(exchange(copies(summed, LINE), LINE), "yh")
    summed = exchange(copies(summed, PLANE), PLANE)
    other = lax.ppermute(summed, "core", [(0, 1), (1, 0)])
    rotation, projected = solve(jnp.stack([core, state]), summed, other, coefficients)
    rotated = rotate(jnp.stack([source for _, source in blocks]), rotation, *(block for block, _ in blocks))
    return (rotated, projected)


def solution(mesh):
    split = Mesh(mesh.devices.reshape(4, 8, 2, 2, 4), ALL)
    placed = (P(GRID, "state"), P(GRID, "state"), P(GRID), P(None, "state"))
    return jax.shard_map(
        shards,
        mesh=split,
        in_specs=placed,
        out_specs=(P(GRID, "state"), P(None, "state")),
        check_vma=False,
    )
```

time: 213 us -> 193 us (0.906); the launches traced: 210 us -> 193 us
  blocking collectives: 129 us -> 66.1 us
  waiting for transfers between devices: 16.9 us -> 57.7 us
  between operations: 14.2 us -> 0.93 us
  starting transfers between devices: 12.4 us -> 25.1 us
  Pallas kernels: 23.6 us -> 27.7 us
    ppermute x2 -> x7, waiting for transfers between devices: 0.43 us -> 57.7 us  [the longest x1 21.3 us: line_blocks(): far = lax.ppermute(across, 'state', [(1, 0), (2, 3)])]
    all_to_all x4 -> x3, blocking collectives: 99.7 us -> 66.1 us  [exchange(): return lax.all_to_all(value, axes, 0, 0, tiled=True)]
    all_to_all x1 -> x0, blocking collectives: 29.3 us -> none  [shards(): x_rows = lax.all_to_all(x_block, 'state', 0, 1, tiled=True)]
    ppermute x2 -> x7, starting transfers between devices: 8.08 us -> 25.1 us  [the longest x1 7.89 us: shards(): other = lax.ppermute(summed, 'core', [(0, 1), (1, 0)])]
    all_to_all x1 -> x0, waiting for transfers between devices: 16.5 us -> none  [shards(): h_rows = lax.all_to_all(after(h_block, x_rows), 'state', 0, 1, tiled=True)]
    all_to_all x1 -> x0, starting transfers between devices: 4.26 us -> none  [shards(): h_rows = lax.all_to_all(after(h_block, x_rows), 'state', 0, 1, tiled=True)]
    pallas_call x1 -> x2, Pallas kernels: 23.6 us -> 27.7 us  [the longest x1 24.4 us: solve(): pl.pallas_call(small_matrices, out_shape=(result, result), in_specs=[pl.B...]
    dot_general x3 -> x4, matrix products: 8.68 us -> 10.5 us  [shards(): product = dot(block, weighted, BY_COLS)]
  transfers between devices with their start and end apart: 4 -> 7, of which waited for: 2 -> 5; matrix products, arithmetic and copies ran while one was open for 4% -> 5% of each run, Pallas kernels for 11% -> 0%
where the time goes in v1:
time: 193 us
  blocking collectives  66.1 us (34%)
  waiting for transfers between devices  57.7 us (30%)
  Pallas kernels  27.7 us (14%)
  starting transfers between devices  25.1 us (13%)
  matrix products  10.5 us (5%)
  other arithmetic  2.79 us (1%)
  local copies, waits for them, and re-layouts  2.1 us (1%)
    all_to_all x3, blocking collectives, exchange(): return lax.all_to_all(value, axes, 0, 0, tiled=True)  66.1 us
    pallas_call x1, Pallas kernels, solve(): pl.pallas_call(small_matrices, out_shape=(result, result), in_specs=[pl.B...  24.4 us
    ppermute x1, waiting for transfers between devices, line_blocks(): far = lax.ppermute(across, 'state', [(1, 0), (2, 3)])  21.3 us
    ppermute x1, waiting for transfers between devices, line_blocks(): pairs = lax.ppermute(x_block, 'state', [(0, 1), (1, 0), (2, 3), (3, 2)])  18.5 us
    ppermute x1, waiting for transfers between devices, line_blocks(): outward = lax.ppermute(middle, 'state', [(1, 0), (2, 3)])  14.5 us
    dot_general x4, matrix products, shards(): product = dot(block, weighted, BY_COLS)  10.5 us
    ppermute x1, starting transfers between devices, shards(): other = lax.ppermute(summed, 'core', [(0, 1), (1, 0)])  7.89 us
    ppermute x1, starting transfers between devices, shards(): summed = kept + lax.ppermute(sent, 'core', [(0, 1), (1, 0)])  5.74 us
  transfers between devices with their start and end apart: 7, of which 5 were waited for; matrix products, arithmetic and copies ran while one was open for 5% of the time, Pallas kernels for 0%

profile of v1, /device:TPU:1, one launch (start us, length us, event | category | flops | bytes accessed | tf_op | source)
XLA Modules:
  0.0 192.9 jit_solution(12624842426157875789)
XLA Ops:
  0.6 1.7 collective-permute-start.1
  2.3 5.6 %collective-permute-start = (f32[2048,128]{1,0:T(8,128)}, f32[2048,128]{1,0:T(8,128)S(1)}, u32[]{:S(2)}, u32[]{:S(2)}) collective-permute-start(f32[2048,128]{1,0:T(8,128)} %refs_0_.1), channel_id=1, source_target_pairs={{0,1},{1,0},{2,3},{3,2},{4,5},{5,4},{6,7},{7,6},{8,9},{9,8},{10,11... | collective-permute-start | bytes 3145736 | tf_op jit(solution)/shard_map/ppermute | solution.py:181
  7.9 0.0 collective-permute-done.1
  7.9 1.3 collective-permute-start.2
  9.2 18.5 %collective-permute-done.refs_1_ = f32[2048,128]{1,0:T(8,128)S(1)} collective-permute-done((f32[2048,128]{1,0:T(8,128)}, f32[2048,128]{1,0:T(8,128)S(1)}, u32[]{:S(2)}, u32[]{:S(2)}) %collective-permute-start) | collective-permute-done | bytes 1048608 | tf_op jit(solution)/shard_map/ppermute | solution.py:181
  27.7 0.0 copy-start.1
  27.7 1.6 collective-permute-start.3
  29.3 0.0 copy-start.4
  29.4 4.1 %convolution_bitcast_fusion.1 = f32[128,256]{1,0:T(8,128)S(1)} fusion(f32[2048,128]{1,0:T(8,128)} %refs_0_.1, f32[2048,128]{1,0:T(8,128)} %param.5, f32[2048]{0:T(1024)} %param.6), kind=kOutput, calls=%fused_computation.2 | convolution fusion | flops 806354944 | bytes 2236416 | tf_op jit(solution)/shard_map/dot_general | solution.py:203
  33.5 0.0 copy-start
  33.5 0.0 copy-start.7
  33.6 0.0 copy-done.1
  33.6 0.0 copy-done.4
  33.6 1.1 copy-done
  34.7 0.0 copy-done.7
  34.7 2.1 %convolution_bitcast_fusion = f32[128,256]{1,0:T(8,128)S(1)} fusion(f32[2048,128]{1,0:T(8,128)S(1)} %collective-permute-done.refs_1_, f32[2048,128]{1,0:T(8,128)S(1)} %copy-done.4, f32[2048,128]{1,0:T(8,128)S(1)} %copy-done, f32[2048]{0:T(1024)S(1)} %copy-done.7), kind=kOutput, calls=%fused_computation.1 | convolution fusion | flops 806354944 | bytes 3284992 | tf_op jit(solution)/shard_map/dot_general | solution.py:203
  36.9 0.0 collective-permute-done.3
  36.9 1.3 collective-permute-start.4
  38.2 14.5 %collective-permute-done.2 = f32[2048,128]{1,0:T(8,128)} collective-permute-done((f32[2048,128]{1,0:T(8,128)}, f32[2048,128]{1,0:T(8,128)}, u32[]{:S(2)}, u32[]{:S(2)}) %collective-permute-start.2) | collective-permute-done | bytes 1048608 | tf_op jit(solution)/shard_map/ppermute | solution.py:183
  52.7 1.3 broadcast_select_fusion.1.refs_2_
  54.0 2.1 %fusion.1 = f32[128,256]{1,0:T(8,128)S(1)} fusion(f32[2048,128]{1,0:T(8,128)S(1)} %broadcast_select_fusion.1.refs_2_, f32[2048,128]{1,0:T(8,128)S(1)} %copy-done.4, f32[2048,128]{1,0:T(8,128)S(1)} %copy-done, f32[2048]{0:T(1024)S(1)} %copy-done.7), kind=kOutput, calls=%fused_computation.4 | convolution fusion | flops 806354944 | bytes 3284992 | tf_op jit(solution)/shard_map/dot_general | solution.py:203
  56.2 0.0 copy-start.5
  56.2 21.3 %collective-permute-done.4 = f32[2048,128]{1,0:T(8,128)S(1)} collective-permute-done((f32[2048,128]{1,0:T(8,128)}, f32[2048,128]{1,0:T(8,128)S(1)}, u32[]{:S(2)}, u32[]{:S(2)}) %collective-permute-start.4) | collective-permute-done | bytes 1048608 | tf_op jit(solution)/shard_map/ppermute | solution.py:185
  77.5 0.1 broadcast_select_fusion.refs_3_
  77.7 0.0 copy-done.5
  77.7 2.1 %fusion = f32[128,256]{1,0:T(8,128)S(1)} fusion(f32[2048,128]{1,0:T(8,128)S(1)} %broadcast_select_fusion.refs_3_, f32[2048,128]{1,0:T(8,128)S(1)} %copy-done.5, f32[2048,128]{1,0:T(8,128)S(1)} %copy-done, f32[2048]{0:T(1024)S(1)} %copy-done.7), kind=kOutput, calls=%fused_computation.3 | convolution fusion | flops 806354944 | bytes 3284992 | tf_op jit(solution)/shard_map/dot_general | solution.py:203
  79.9 0.0 copy-start.6
  79.9 0.8 copy-done.6
  80.7 5.7 %collective-permute-start.5 = (f32[512,128]{1,0:T(8,128)S(1)}, f32[512,128]{1,0:T(8,128)}, u32[]{:S(2)}, u32[]{:S(2)}) collective-permute-start(f32[512,128]{1,0:T(8,128)S(1)} %dynamic-slice_bitcast_fusion), channel_id=1, source_target_pairs={{0,4},{4,0},{1,5},{5,1},{2,6},{6,2},{3,7},{7,3},{8,12},{12,8},{9,1... | collective-permute-start | bytes 786440 | tf_op jit(solution)/shard_map/ppermute | solution.py:210
  86.4 1.3 collective-permute-done.5
  87.7 1.1 bitcast_add_fusion
  88.8 23.2 %all_to_all.23 = f32[32,16,128]{2,1,0:T(8,128)S(1)} all-to-all(f32[32,16,128]{2,1,0:T(8,128)S(1)} %bitcast.67), channel_id=1, replica_groups=mesh['x'=4,'z'=8,'yh'=2,'core'=2,'state'=4] {'x','z'}, dimensions={0} | all-to-all | bytes 524288 | tf_op jit(solution)/shard_map/all_to_all | solution.py:25
  112.0 12.8 %all_to_all.24 = f32[8,16,128]{2,1,0:T(8,128)S(1)} all-to-all(f32[8,16,128]{2,1,0:T(8,128)S(1)} %broadcast_in_dim.27), channel_id=1, replica_groups=mesh['x'=4,'z'=8,'yh'=2,'core'=2,'state'=4] {'yh','state'}, dimensions={0} | all-to-all | bytes 131072 | tf_op jit(solution)/shard_map/all_to_all | solution.py:25
  124.7 0.1 broadcast_in_dim.28
  124.8 0.0 copy-start.3
  124.9 30.2 %all_to_all.25 = f32[32,64,128]{2,1,0:T(8,128)S(1)} all-to-all(f32[32,64,128]{2,1,0:T(8,128)S(1)} %broadcast_in_dim.28), channel_id=1, replica_groups=mesh['x'=4,'z'=8,'yh'=2,'core'=2,'state'=4] {'x','z'}, dimensions={0} | all-to-all | bytes 2097152 | tf_op jit(solution)/shard_map/all_to_all | solution.py:25
  155.1 7.9 %collective-permute-start.6 = (f32[2048,128]{1,0:T(8,128)S(1)}, f32[2048,128]{1,0:T(8,128)S(1)}, u32[]{:S(2)}, u32[]{:S(2)}) collective-permute-start(f32[2048,128]{1,0:T(8,128)S(1)} %bitcast.63), channel_id=1, source_target_pairs={{0,4},{4,0},{1,5},{5,1},{2,6},{6,2},{3,7},{7,3},{8,12},{12,8},{9,1... | collective-permute-start | bytes 3145736 | tf_op jit(solution)/shard_map/ppermute | solution.py:214
  163.0 0.1 pad_add_fusion.1.place_ref
  163.1 0.1 pad_add_fusion.source_ref
  163.1 0.0 copy-start.2
  163.1 2.1 %collective-permute-done.6.other_packed = f32[2048,128]{1,0:T(8,128)S(1)} collective-permute-done((f32[2048,128]{1,0:T(8,128)S(1)}, f32[2048,128]{1,0:T(8,128)S(1)}, u32[]{:S(2)}, u32[]{:S(2)}) %collective-permute-start.6) | collective-permute-done | bytes 1048608 | tf_op jit(solution)/shard_map/ppermute | solution.py:214
  165.3 0.0 copy-done.3
  165.3 24.4 %shard_map.59 = (f32[512,128]{1,0:T(8,128)S(1)}, f32[512,128]{1,0:T(8,128)}) custom-call(s32[2]{0:T(128)S(1)} %pad_add_fusion.1.place_ref, f32[2048,128]{1,0:T(8,128)S(1)} %bitcast.64, f32[2048,128]{1,0:T(8,128)S(1)} %collective-permute-done.6.other_packed, f32[512,128]{1,0:T(8,128)S(1)} %copy-done.3), custom_call_target="tpu_custom_call" | custom-call | flops 20000000000 | bytes 4194304 | tf_op jit(solution)/shard_map/pallas_call | solution.py:133
  189.6 0.0 copy-done.2
  189.6 3.3 %shard_map.60 = f32[2048,128]{1,0:T(8,128)} custom-call(s32[4]{0:T(128)S(1)} %pad_add_fusion.source_ref, f32[512,128]{1,0:T(8,128)S(1)} %get-tuple-element.4.rotation_ref, f32[2048,128]{1,0:T(8,128)S(1)} %copy-done, f32[2048,128]{1,0:T(8,128)S(1)} %copy-done.2, f32[2048,128]{1,0:T(8,128)S(1)} %broadcast_select_fusion.1.refs_2_, ...), custom_call_target="tpu_custom_call" | custom-call | flops 2000000000 | bytes 6291456 | tf_op jit(solution)/shard_map/pallas_call | solution.py:165
  (13 shorter events, 0.2 us)
Async XLA Ops:
  0.6 7.3 %collective-permute-start.1 = (f32[2048,128]{1,0:T(8,128)}, f32[2048,128]{1,0:T(8,128)}, u32[]{:S(2)}, u32[]{:S(2)}) collective-permute-start(f32[2048,128]{1,0:T(8,128)} %refs_0_.1), channel_id=1, source_target_pairs={{1,2},{2,1},{5,6},{6,5},{9,10},{10,9},{13,14},{14,13},{17,18},{18,... | collective-permute-start | bytes 3145736 | tf_op jit(solution)/shard_map/ppermute | solution.py:182
  2.3 25.4 %collective-permute-start = (f32[2048,128]{1,0:T(8,128)}, f32[2048,128]{1,0:T(8,128)S(1)}, u32[]{:S(2)}, u32[]{:S(2)}) collective-permute-start(f32[2048,128]{1,0:T(8,128)} %refs_0_.1), channel_id=1, source_target_pairs={{0,1},{1,0},{2,3},{3,2},{4,5},{5,4},{6,7},{7,6},{8,9},{9,8},{10,11... | collective-permute-start | bytes 3145736 | tf_op jit(solution)/shard_map/ppermute | solution.py:181
  7.9 44.8 %collective-permute-start.2 = (f32[2048,128]{1,0:T(8,128)}, f32[2048,128]{1,0:T(8,128)}, u32[]{:S(2)}, u32[]{:S(2)}) collective-permute-start(f32[2048,128]{1,0:T(8,128)} %collective-permute-done.1), channel_id=1, source_target_pairs={{1,0},{2,3},{5,4},{6,7},{9,8},{10,11},{13,12},{14,15},{17,16},{18,... | collective-permute-start | bytes 3145736 | tf_op jit(solution)/shard_map/ppermute | solution.py:183
  27.7 5.9 %copy-start.1 = (f32[2048,128]{1,0:T(8,128)}, f32[2048,128]{1,0:T(8,128)S(1)}, u32[]{:S(2)}) copy-start(f32[2048,128]{1,0:T(8,128)S(1)} %collective-permute-done.refs_1_) | copy-start | bytes 3145732
  27.7 9.2 %collective-permute-start.3 = (f32[2048,128]{1,0:T(8,128)S(1)}, f32[2048,128]{1,0:T(8,128)}, u32[]{:S(2)}, u32[]{:S(2)}) collective-permute-start(f32[2048,128]{1,0:T(8,128)S(1)} %collective-permute-done.refs_1_), channel_id=1, source_target_pairs={{1,2},{2,1},{5,6},{6,5},{9,10},{10,9},{13,14},{14,13},{17,18},{18,... | collective-permute-start | bytes 3145736 | tf_op jit(solution)/shard_map/ppermute | solution.py:184
  29.3 4.3 %copy-start.4 = (f32[2048,128]{1,0:T(8,128)S(1)}, f32[2048,128]{1,0:T(8,128)}, u32[]{:S(2)}) copy-start(f32[2048,128]{1,0:T(8,128)} %param.5) | copy-start | bytes 3145732
  33.5 1.2 copy-start
  33.5 1.2 copy-start.7
  36.9 40.6 %collective-permute-start.4 = (f32[2048,128]{1,0:T(8,128)}, f32[2048,128]{1,0:T(8,128)S(1)}, u32[]{:S(2)}, u32[]{:S(2)}) collective-permute-start(f32[2048,128]{1,0:T(8,128)} %collective-permute-done.3), channel_id=1, source_target_pairs={{1,0},{2,3},{5,4},{6,7},{9,8},{10,11},{13,12},{14,15},{17,16},{18,... | collective-permute-start | bytes 3145736 | tf_op jit(solution)/shard_map/ppermute | solution.py:185
  56.2 21.5 %copy-start.5 = (f32[2048,128]{1,0:T(8,128)S(1)}, f32[2048,128]{1,0:T(8,128)}, u32[]{:S(2)}) copy-start(f32[2048,128]{1,0:T(8,128)} %param.5) | copy-start | bytes 3145732
  79.9 0.8 copy-start.6
  80.7 7.0 %collective-permute-start.5 = (f32[512,128]{1,0:T(8,128)S(1)}, f32[512,128]{1,0:T(8,128)}, u32[]{:S(2)}, u32[]{:S(2)}) collective-permute-start(f32[512,128]{1,0:T(8,128)S(1)} %dynamic-slice_bitcast_fusion), channel_id=1, source_target_pairs={{0,4},{4,0},{1,5},{5,1},{2,6},{6,2},{3,7},{7,3},{8,12},{12,8},{9,1... | collective-permute-start | bytes 786440 | tf_op jit(solution)/shard_map/ppermute | solution.py:210
  124.8 40.4 %copy-start.3 = (f32[512,128]{1,0:T(8,128)S(1)}, f32[512,128]{1,0:T(8,128)}, u32[]{:S(2)}) copy-start(f32[512,128]{1,0:T(8,128)} %coefficients.1) | copy-start | bytes 786436
  155.1 10.2 %collective-permute-start.6 = (f32[2048,128]{1,0:T(8,128)S(1)}, f32[2048,128]{1,0:T(8,128)S(1)}, u32[]{:S(2)}, u32[]{:S(2)}) collective-permute-start(f32[2048,128]{1,0:T(8,128)S(1)} %bitcast.63), channel_id=1, source_target_pairs={{0,4},{4,0},{1,5},{5,1},{2,6},{6,2},{3,7},{7,3},{8,12},{12,8},{9,1... | collective-permute-start | bytes 3145736 | tf_op jit(solution)/shard_map/ppermute | solution.py:214
  163.1 26.5 %copy-start.2 = (f32[2048,128]{1,0:T(8,128)S(1)}, f32[2048,128]{1,0:T(8,128)}, u32[]{:S(2)}) copy-start(f32[2048,128]{1,0:T(8,128)} %copy-done.1) | copy-start | bytes 3145732

commit v2 on v1

--- a/solution.py
+++ b/solution.py
@@ -13,6 +13,7 @@
 LINE = ("yh", "state")
 HIGHEST = lax.Precision.HIGHEST
 EDGE, SUB, RUN = 128, 8, 16
+ROW_ORDER = ((1, 0, 2, 3), (2, 3, 1, 0))
 dot = functools.partial(lax.dot_general, precision=HIGHEST, preferred_element_type=jnp.float32)
 PLAIN, BY_ROWS, BY_COLS = (((1,), (0,)), ((), ())), (((1,), (1,)), ((), ())), (((0,), (0,)), ((), ()))
 
@@ -68,12 +69,13 @@
     return right
 
 
-def unpack(packed, states, matrix):
-    nb = matrix.shape[0]
-    for first in range(0, nb, RUN):
-        for t in range(states):
-            at = first * states + t * RUN
-            matrix[first : first + RUN, EDGE * t : EDGE * (t + 1)] = packed[at : at + RUN, :]
+def unpack(packed, matrix):
+    panels = matrix.shape[1] // EDGE
+    for run in range(matrix.shape[0] // RUN):
+        for panel in range(panels):
+            at = (run * panels + panel) * RUN
+            first = ROW_ORDER[panel // 2][run * RUN // EDGE] * EDGE + run * RUN % EDGE
+            matrix[first : first + RUN, EDGE * panel : EDGE * (panel + 1)] = packed[at : at + RUN, :]
 
 
 def small_matrices(place_ref, own_packed, other_packed, coefficients, rotation_ref, projected_ref, work, hamil, inverse, block):
@@ -83,13 +85,13 @@
 
     @pl.when(place_ref[0] == 0)
     def _():
-        unpack(own_packed, blocks, work)
-        unpack(other_packed, blocks, hamil)
+        unpack(own_packed, work)
+        unpack(other_packed, hamil)
 
     @pl.when(place_ref[0] != 0)
     def _():
-        unpack(other_packed, blocks, work)
-        unpack(own_packed, blocks, hamil)
+        unpack(other_packed, work)
+        unpack(own_packed, hamil)
 
     @pl.loop(0, blocks)
     def _(k):
@@ -146,22 +148,29 @@
     return high, (value - high.astype(jnp.float32)).astype(jnp.bfloat16)
 
 
-def rotate_rows(source_ref, rotation_ref, *refs):
-    *block_refs, rotated_ref = refs
-    rows = [
-        rotation_ref[pl.ds(pl.multiple_of(source_ref[b] * EDGE, EDGE), EDGE), :] for b in range(len(block_refs))
-    ]
+def rotate_rows(source_ref, rotation_ref, own, pairs, middle, outward, across, far, rotated_ref):
+    rows = [rotation_ref[pl.ds(pl.multiple_of(source_ref[b] * EDGE, EDGE), EDGE), :] for b in range(4)]
     turn_high, turn_low = high_low(jnp.concatenate(rows, axis=0))
-    high, low = high_low(jnp.concatenate([ref[...] for ref in block_refs], axis=1))
+    at_end = source_ref[4] == 1
+    third, fourth = jnp.where(at_end, outward[...], middle[...]), jnp.where(at_end, far[...], across[...])
+    high, low = high_low(jnp.concatenate([own[...], pairs[...], third, fourth], axis=1))
     wide = jnp.dot(high, jnp.concatenate([turn_high, turn_low], axis=1), preferred_element_type=jnp.float32)
     small = wide[:, EDGE:] + jnp.dot(low, turn_high, preferred_element_type=jnp.float32)
     rotated_ref[...] = wide[:, :EDGE] + small
 
 
-def rotate(sources, rotation, *blocks):
+def rotate(state, rotation, *blocks):
     rows, width = blocks[0].shape
     tile = rows // 4
     by_rows = pl.BlockSpec((tile, width), lambda i: (i, 0))
+    at_end = (state == 0) | (state == 3)
+    sources = [
+        state,
+        state + 1 - 2 * (state % 2),
+        jnp.where(state < 2, 2, 1),
+        jnp.where(state < 2, 3, 0),
+        at_end.astype(jnp.int32),
+    ]
     return pl.pallas_call(
         rotate_rows,
         grid=(rows // tile,),
@@ -172,48 +181,49 @@
             *[by_rows] * len(blocks),
         ],
         out_specs=by_rows,
-        cost_estimate=pl.CostEstimate(flops=2 * 10**9, bytes_accessed=6 * 2**20, transcendentals=0),
+        cost_estimate=pl.CostEstimate(flops=2 * 10**9, bytes_accessed=8 * 2**20, transcendentals=0),
         compiler_params=pltpu.CompilerParams(vmem_limit_bytes=32 * 2**20),
-    )(sources, rotation, *blocks)
-
-
-def line_blocks(x_block, state):
-    pairs = lax.ppermute(x_block, "state", [(0, 1), (1, 0), (2, 3), (3, 2)])
-    middle = lax.ppermute(x_block, "state", [(1, 2), (2, 1)])
-    outward = lax.ppermute(middle, "state", [(1, 0), (2, 3)])
-    across = lax.ppermute(pairs, "state", [(1, 2), (2, 1)])
-    far = lax.ppermute(across, "state", [(1, 0), (2, 3)])
-    at_end = (state == 0) | (state == 3)
-    return (
-        (x_block, state),
-        (pairs, state + 1 - 2 * (state % 2)),
-        (jnp.where(at_end, outward, middle), jnp.where(state < 2, 2, 1)),
-        (jnp.where(at_end, far, across), jnp.where(state < 2, 3, 0)),
-    )
+    )(jnp.stack(sources), rotation, *blocks)
 
 
 def shards(x_block, h_block, mass_weights, coefficients):
     state, core = lax.axis_index("state"), lax.axis_index("core")
     width = x_block.shape[1]
-    blocks = line_blocks(x_block, state)
-    weighted = mass_weights[:, None] * jnp.concatenate([x_block, h_block], axis=1)
-
-    parts = jnp.zeros((2, len(blocks), width, width), jnp.float32)
-    for block, source in blocks:
-        product = dot(block, weighted, BY_COLS)
-        product = jnp.stack([product[:, :width], product[:, width:]])
-        parts = lax.dynamic_update_slice_in_dim(parts, product[:, None], source, 1)
-    parts = parts.reshape(2, -1, width)
-
-    kept = lax.dynamic_index_in_dim(parts, core, 0, keepdims=False)
-    sent = lax.dynamic_index_in_dim(parts, 1 - core, 0, keepdims=False)
+    send = functools.partial(lax.ppermute, axis_name="state")
+
+    pairs = send(x_block, perm=[(0, 1), (1, 0), (2, 3), (3, 2)])
+    middle = send(x_block, perm=[(1, 2), (2, 1)])
+    across = send(pairs, perm=[(1, 2), (2, 1)])
+    outer_h = send(after(h_block, pairs), perm=[(0, 1), (3, 2)])
+    outward = send(middle, perm=[(1, 0), (2, 3)])
+    far = send(across, perm=[(1, 0), (2, 3)])
+    times = functools.partial(
+        lax.dot_general,
+        dimension_numbers=BY_COLS,
+        precision=lax.Precision.HIGH,
+        preferred_element_type=jnp.float32,
+    )
+    near = jnp.concatenate([x_block, pairs, middle], axis=1)
+    early = mass_weights[:, None] * jnp.concatenate([pairs, x_block, h_block], axis=1)
+    late = mass_weights[:, None] * outer_h
+    near_early, near_late = times(near, early), times(near, late)
+    far_early, far_late = times(across, early), times(across, late)
+    gram = jnp.concatenate([near_early[:, : 2 * width], far_early[:, : 2 * width]], axis=0)
+    hamil_outer = jnp.concatenate([near_late, far_late], axis=0)
+    hamil_own = jnp.concatenate([near_early[:, 2 * width :], far_early[:, 2 * width :]], axis=0)
+    hamil = jnp.concatenate([hamil_outer, hamil_own], axis=1)
+
+    kept, sent = jnp.where(core == 0, gram, hamil), jnp.where(core == 0, hamil, gram)
     summed = kept + lax.ppermute(sent, "core", [(0, 1), (1, 0)])
-    summed = total(exchange(summed, PLANE), PLANE)
-    summed = total(exchange(copies(summed, LINE), LINE), "yh")
-    summed = exchange(copies(summed, PLANE), PLANE)
+    summed = total(exchange(after(summed, outward), PLANE), PLANE)
+    summed = after(summed, far)
+    shape = (lax.axis_size("yh"), lax.axis_size("state")) + summed.shape
+    summed = jnp.sum(exchange(copies(summed, LINE), LINE).reshape(shape), axis=0)
+    panels = summed[1][:, :width], summed[1][:, width:], summed[2][:, width:], summed[2][:, :width]
+    summed = exchange(copies(jnp.concatenate(panels, axis=0), PLANE), PLANE)
     other = lax.ppermute(summed, "core", [(0, 1), (1, 0)])
     rotation, projected = solve(jnp.stack([core, state]), summed, other, coefficients)
-    rotated = rotate(jnp.stack([source for _, source in blocks]), rotation, *(block for block, _ in blocks))
+    rotated = rotate(state, rotation, x_block, pairs, middle, outward, across, far)
     return (rotated, projected)
 
 

time: 193 us -> 186 us (0.964)
  waiting for transfers between devices: 57.7 us -> 33.6 us
  blocking collectives: 66.1 us -> 72.9 us
  starting transfers between devices: 25.1 us -> 30.7 us
  Pallas kernels: 27.7 us -> 29.8 us
    ppermute x5 -> x6, waiting for transfers between devices: 54.3 us -> 31 us  [the longest x1 17.8 us: shards(): pairs = send(x_block, perm=[(0, 1), (1, 0), (2, 3), (3, 2)])]
    all_to_all x3, blocking collectives: 66.1 us -> 72.9 us  [exchange(): return lax.all_to_all(value, axes, 0, 0, tiled=True)]
    ppermute x5 -> x6, starting transfers between devices: 11.5 us -> 18.1 us  [the longest x1 9.15 us: shards(): outer_h = send(after(h_block, pairs), perm=[(0, 1), (3, 2)])]
  transfers between devices with their start and end apart: 7 -> 8, of which waited for: 5 -> 4; matrix products, arithmetic and copies ran while one was open for 5% -> 8% of each run, Pallas kernels for 0% -> 0%
where the time goes in v2:
time: 186 us; the launch traced here: 185 us
  blocking collectives  72.9 us (39%)
  waiting for transfers between devices  33.6 us (18%)
  starting transfers between devices  30.7 us (17%)
  Pallas kernels  29.8 us (16%)
  matrix products  11.6 us (6%)
  local copies, waits for them, and re-layouts  3.43 us (2%)
  other arithmetic  1.99 us (1%)
    all_to_all x3, blocking collectives, exchange(): return lax.all_to_all(value, axes, 0, 0, tiled=True)  72.9 us
    pallas_call x1, Pallas kernels, solve(): pl.pallas_call(small_matrices, out_shape=(result, result), in_specs=[pl.B...  25.4 us
    ppermute x1, waiting for transfers between devices, shards(): pairs = send(x_block, perm=[(0, 1), (1, 0), (2, 3), (3, 2)])  17.8 us
    ppermute x1, waiting for transfers between devices, shards(): outer_h = send(after(h_block, pairs), perm=[(0, 1), (3, 2)])  13.1 us
    ppermute x1, starting transfers between devices, shards(): outer_h = send(after(h_block, pairs), perm=[(0, 1), (3, 2)])  9.15 us
    ppermute x1, starting transfers between devices, shards(): other = lax.ppermute(summed, 'core', [(0, 1), (1, 0)])  7.87 us
    dot_general x2, matrix products, shards(): near_early, near_late = (times(near, early), times(near, late))  6.29 us
    dot_general x2, matrix products, shards(): far_early, far_late = (times(across, early), times(across, late))  5.29 us
  transfers between devices with their start and end apart: 8, of which 4 were waited for; matrix products, arithmetic and copies ran while one was open for 8% of the time, Pallas kernels for 0%

profile of v2, /device:TPU:1, one launch (start us, length us, event | category | flops | bytes accessed | tf_op | source)
XLA Modules:
  0.0 184.8 jit_solution(2764911600194259402)
XLA Ops:
  0.6 4.0 %collective-permute-start = (f32[2048,128]{1,0:T(8,128)}, f32[2048,128]{1,0:T(8,128)S(1)}, u32[]{:S(2)}, u32[]{:S(2)}) collective-permute-start(f32[2048,128]{1,0:T(8,128)} %own.1), channel_id=1, source_target_pairs={{0,1},{1,0},{2,3},{3,2},{4,5},{5,4},{6,7},{7,6},{8,9},{9,8},{10,11... | collective-permute-start | bytes 3145736 | tf_op jit(solution)/shard_map/ppermute | solution.py:194
  4.7 0.7 collective-permute-start.1
  5.4 0.0 copy-start
  5.4 0.0 copy-start.4
  5.4 0.0 copy-start.5
  5.4 17.8 %collective-permute-done.pairs = f32[2048,128]{1,0:T(8,128)S(1)} collective-permute-done((f32[2048,128]{1,0:T(8,128)}, f32[2048,128]{1,0:T(8,128)S(1)}, u32[]{:S(2)}, u32[]{:S(2)}) %collective-permute-start) | collective-permute-done | bytes 1048608 | tf_op jit(solution)/shard_map/ppermute | solution.py:194
  23.3 1.6 collective-permute-start.2
  24.9 1.3 constant_dynamic-update-slice_fusion.2
  26.2 9.2 %collective-permute-start.3 = (f32[2048,128]{1,0:T(8,128)}, f32[2048,128]{1,0:T(8,128)S(1)}, u32[]{:S(2)}, u32[]{:S(2)}) collective-permute-start(f32[2048,128]{1,0:T(8,128)} %param.5), channel_id=1, source_target_pairs={{0,1},{3,2},{4,5},{7,6},{8,9},{11,10},{12,13},{15,14},{16,17},{19,... | collective-permute-start | bytes 3145736 | tf_op jit(solution)/shard_map/ppermute | solution.py:197
  35.4 0.1 constant_dynamic-update-slice_fusion.1
  35.4 0.0 collective-permute-done.1.middle
  35.5 0.1 constant_dynamic-update-slice_fusion
  35.5 0.0 copy-done
  35.5 0.0 copy-done.4
  35.6 0.0 copy-done.5
  35.6 3.3 %fusion.1 = f32[384,384]{1,0:T(8,128)S(1)} fusion(f32[2048,384]{1,0:T(8,128)S(1)} %constant_dynamic-update-slice_fusion, f32[2048,128]{1,0:T(8,128)S(1)} %copy-done.4, f32[2048,128]{1,0:T(8,128)S(1)} %copy-done, f32[2048,128]{1,0:T(8,128)S(1)} %collective-permute-done.pairs, f32[2048]{0:T(1024)S(1)} %copy-done.5), kind=kOutput, calls=%fused_computation.2 | convolution fusion | flops 1814298624 | bytes 6889472 | tf_op jit(solution)/shard_map/dot_general | solution.py:209
  39.0 1.3 collective-permute-start.5
  40.3 0.0 collective-permute-done.2.across
  40.3 2.8 %fusion.4 = f32[128,384]{1,0:T(8,128)S(1)} fusion(f32[2048,128]{1,0:T(8,128)} %collective-permute-done.2.across, f32[2048,128]{1,0:T(8,128)S(1)} %copy-done.4, f32[2048,128]{1,0:T(8,128)S(1)} %copy-done, f32[2048,128]{1,0:T(8,128)S(1)} %collective-permute-done.pairs, f32[2048]{0:T(1024)S(1)} %copy-done.5), kind=kOutput, calls=%fused_computation.5 | convolution fusion | flops 606339072 | bytes 4399104 | tf_op jit(solution)/shard_map/dot_general | solution.py:210
  43.1 13.1 %collective-permute-done.3 = f32[2048,128]{1,0:T(8,128)S(1)} collective-permute-done((f32[2048,128]{1,0:T(8,128)}, f32[2048,128]{1,0:T(8,128)S(1)}, u32[]{:S(2)}, u32[]{:S(2)}) %collective-permute-start.3) | collective-permute-done | bytes 1048608 | tf_op jit(solution)/shard_map/ppermute | solution.py:197
  56.2 2.9 %fusion.6 = f32[384,128]{1,0:T(8,128)S(1)} fusion(f32[2048,384]{1,0:T(8,128)S(1)} %constant_dynamic-update-slice_fusion, f32[2048,128]{1,0:T(8,128)S(1)} %collective-permute-done.3, f32[2048]{0:T(1024)S(1)} %copy-done.5), kind=kOutput, calls=%fused_computation.8 | convolution fusion | flops 604241920 | bytes 4399104 | tf_op jit(solution)/shard_map/dot_general | solution.py:209
  59.2 2.5 %convolution_bitcast_fusion = f32[128,128]{1,0:T(8,128)S(1)} fusion(f32[2048,128]{1,0:T(8,128)} %collective-permute-done.2.across, f32[2048,128]{1,0:T(8,128)S(1)} %collective-permute-done.3, f32[2048]{0:T(1024)S(1)} %copy-done.5), kind=kOutput, calls=%fused_computation.6 | convolution fusion | flops 201588736 | bytes 2170880 | tf_op jit(solution)/shard_map/dot_general | solution.py:210
  61.7 0.1 fusion.10
  61.8 4.7 %collective-permute-start.4 = (f32[512,256]{1,0:T(8,128)S(1)}, f32[512,256]{1,0:T(8,128)S(1)}, u32[]{:S(2)}, u32[]{:S(2)}) collective-permute-start(f32[512,256]{1,0:T(8,128)S(1)} %fusion.10), channel_id=1, source_target_pairs={{0,4},{4,0},{1,5},{5,1},{2,6},{6,2},{3,7},{7,3},{8,12},{12,8},{9,1... | collective-permute-start | bytes 1572872 | tf_op jit(solution)/shard_map/ppermute | solution.py:217
  66.4 1.3 collective-permute-start.6
  67.7 0.2 collective-permute-done.4
  68.0 0.1 select_add_fusion
  68.1 0.0 copy-start.3
  68.1 0.0 collective-permute-done.5.outward
  68.1 0.0 copy-start.1
  68.1 1.0 copy-done.1
  69.1 26.9 %all_to_all.23 = f32[32,16,256]{2,1,0:T(8,128)} all-to-all(f32[32,16,256]{2,1,0:T(8,128)S(1)} %bitcast.21), channel_id=1, replica_groups=mesh['x'=4,'z'=8,'yh'=2,'core'=2,'state'=4] {'x','z'}, dimensions={0} | all-to-all | bytes 1048576 | tf_op jit(solution)/shard_map/all_to_all | solution.py:26
  96.0 1.1 reduce_sum.18
  97.1 0.0 collective-permute-done.6.far
  97.1 14.3 %all_to_all.24 = f32[8,16,256]{2,1,0:T(8,128)S(1)} all-to-all(f32[8,16,256]{2,1,0:T(8,128)S(1)} %broadcast_in_dim.8), channel_id=1, replica_groups=mesh['x'=4,'z'=8,'yh'=2,'core'=2,'state'=4] {'yh','state'}, dimensions={0} | all-to-all | bytes 262144 | tf_op jit(solution)/shard_map/all_to_all | solution.py:26
  111.4 0.6 reduce_sum.19
  112.0 0.7 slice_bitcast_fusion.1
  112.8 0.1 broadcast_in_dim.9
  112.9 31.6 %all_to_all.25 = f32[32,64,128]{2,1,0:T(8,128)} all-to-all(f32[32,64,128]{2,1,0:T(8,128)S(1)} %broadcast_in_dim.9), channel_id=1, replica_groups=mesh['x'=4,'z'=8,'yh'=2,'core'=2,'state'=4] {'x','z'}, dimensions={0} | all-to-all | bytes 2097152 | tf_op jit(solution)/shard_map/all_to_all | solution.py:26
  144.6 7.9 %collective-permute-start.7 = (f32[2048,128]{1,0:T(8,128)}, f32[2048,128]{1,0:T(8,128)}, u32[]{:S(2)}, u32[]{:S(2)}) collective-permute-start(f32[2048,128]{1,0:T(8,128)} %bitcast.12.own_packed), channel_id=1, source_target_pairs={{0,4},{4,0},{1,5},{5,1},{2,6},{6,2},{3,7},{7,3},{8,12},{12,8},{9,1... | collective-permute-start | bytes 3145736 | tf_op jit(solution)/shard_map/ppermute | solution.py:224
  152.5 0.1 stack.34.source_ref
  152.6 0.1 pad_add_fusion.place_ref
  152.6 0.0 copy-start.2
  152.6 2.4 %collective-permute-done.7.other_packed = f32[2048,128]{1,0:T(8,128)} collective-permute-done((f32[2048,128]{1,0:T(8,128)}, f32[2048,128]{1,0:T(8,128)}, u32[]{:S(2)}, u32[]{:S(2)}) %collective-permute-start.7) | collective-permute-done | bytes 1048608 | tf_op jit(solution)/shard_map/ppermute | solution.py:224
  155.0 0.0 copy-done.3
  155.1 25.4 %shard_map.59 = (f32[512,128]{1,0:T(8,128)S(1)}, f32[512,128]{1,0:T(8,128)}) custom-call(s32[2]{0:T(128)S(1)} %pad_add_fusion.place_ref, f32[2048,128]{1,0:T(8,128)} %bitcast.12.own_packed, f32[2048,128]{1,0:T(8,128)} %collective-permute-done.7.other_packed, f32[512,128]{1,0:T(8,128)S(1)} %copy-done.3), custom_call_target="tpu_custom_call" | custom-call | flops 20000000000 | bytes 4194304 | tf_op jit(solution)/shard_map/pallas_call | solution.py:135
  180.4 0.0 copy-done.2
  180.4 4.4 %shard_map.60 = f32[2048,128]{1,0:T(8,128)} custom-call(s32[5]{0:T(128)S(1)} %stack.34.source_ref, f32[512,128]{1,0:T(8,128)S(1)} %get-tuple-element.10.rotation_ref, f32[2048,128]{1,0:T(8,128)S(1)} %copy-done, f32[2048,128]{1,0:T(8,128)S(1)} %collective-permute-done.pairs, f32[2048,128]{1,0:T(8,128)S(1)} %collective-permute-done.1.middle, ...), custom_call_target="tpu_custom_call" | custom-call | flops 2000000000 | bytes 8388608 | tf_op jit(solution)/shard_map/pallas_call | solution.py:174
  (7 shorter events, 0.1 us)
Async XLA Ops:
  0.6 22.7 %collective-permute-start = (f32[2048,128]{1,0:T(8,128)}, f32[2048,128]{1,0:T(8,128)S(1)}, u32[]{:S(2)}, u32[]{:S(2)}) collective-permute-start(f32[2048,128]{1,0:T(8,128)} %own.1), channel_id=1, source_target_pairs={{0,1},{1,0},{2,3},{3,2},{4,5},{5,4},{6,7},{7,6},{8,9},{9,8},{10,11... | collective-permute-start | bytes 3145736 | tf_op jit(solution)/shard_map/ppermute | solution.py:194
  4.7 30.8 %collective-permute-start.1 = (f32[2048,128]{1,0:T(8,128)}, f32[2048,128]{1,0:T(8,128)S(1)}, u32[]{:S(2)}, u32[]{:S(2)}) collective-permute-start(f32[2048,128]{1,0:T(8,128)} %own.1), channel_id=1, source_target_pairs={{1,2},{2,1},{5,6},{6,5},{9,10},{10,9},{13,14},{14,13},{17,18},{18,... | collective-permute-start | bytes 3145736 | tf_op jit(solution)/shard_map/ppermute | solution.py:195
  5.4 30.1 %copy-start = (f32[2048,128]{1,0:T(8,128)S(1)}, f32[2048,128]{1,0:T(8,128)}, u32[]{:S(2)}) copy-start(f32[2048,128]{1,0:T(8,128)} %own.1) | copy-start | bytes 3145732
  5.4 30.1 %copy-start.4 = (f32[2048,128]{1,0:T(8,128)S(1)}, f32[2048,128]{1,0:T(8,128)}, u32[]{:S(2)}) copy-start(f32[2048,128]{1,0:T(8,128)} %param.5) | copy-start | bytes 3145732
  5.4 30.1 %copy-start.5 = (f32[2048]{0:T(1024)S(1)}, f32[2048]{0:T(1024)}, u32[]{:S(2)}) copy-start(f32[2048]{0:T(1024)} %param.6) | copy-start | bytes 24580
  23.3 17.0 %collective-permute-start.2 = (f32[2048,128]{1,0:T(8,128)S(1)}, f32[2048,128]{1,0:T(8,128)}, u32[]{:S(2)}, u32[]{:S(2)}) collective-permute-start(f32[2048,128]{1,0:T(8,128)S(1)} %collective-permute-done.pairs), channel_id=1, source_target_pairs={{1,2},{2,1},{5,6},{6,5},{9,10},{10,9},{13,14},{14,13},{17,18},{18,... | collective-permute-start | bytes 3145736 | tf_op jit(solution)/shard_map/ppermute | solution.py:196
  26.2 30.0 %collective-permute-start.3 = (f32[2048,128]{1,0:T(8,128)}, f32[2048,128]{1,0:T(8,128)S(1)}, u32[]{:S(2)}, u32[]{:S(2)}) collective-permute-start(f32[2048,128]{1,0:T(8,128)} %param.5), channel_id=1, source_target_pairs={{0,1},{3,2},{4,5},{7,6},{8,9},{11,10},{12,13},{15,14},{16,17},{19,... | collective-permute-start | bytes 3145736 | tf_op jit(solution)/shard_map/ppermute | solution.py:197
  39.0 29.1 %collective-permute-start.5 = (f32[2048,128]{1,0:T(8,128)S(1)}, f32[2048,128]{1,0:T(8,128)S(1)}, u32[]{:S(2)}, u32[]{:S(2)}) collective-permute-start(f32[2048,128]{1,0:T(8,128)S(1)} %collective-permute-done.1.middle), channel_id=1, source_target_pairs={{1,0},{2,3},{5,4},{6,7},{9,8},{10,11},{13,12},{14,15},{17,16},{18,... | collective-permute-start | bytes 3145736 | tf_op jit(solution)/shard_map/ppermute | solution.py:198
  61.8 6.2 %collective-permute-start.4 = (f32[512,256]{1,0:T(8,128)S(1)}, f32[512,256]{1,0:T(8,128)S(1)}, u32[]{:S(2)}, u32[]{:S(2)}) collective-permute-start(f32[512,256]{1,0:T(8,128)S(1)} %fusion.10), channel_id=1, source_target_pairs={{0,4},{4,0},{1,5},{5,1},{2,6},{6,2},{3,7},{7,3},{8,12},{12,8},{9,1... | collective-permute-start | bytes 1572872 | tf_op jit(solution)/shard_map/ppermute | solution.py:217
  66.4 30.6 %collective-permute-start.6 = (f32[2048,128]{1,0:T(8,128)}, f32[2048,128]{1,0:T(8,128)}, u32[]{:S(2)}, u32[]{:S(2)}) collective-permute-start(f32[2048,128]{1,0:T(8,128)} %collective-permute-done.2.across), channel_id=1, source_target_pairs={{1,0},{2,3},{5,4},{6,7},{9,8},{10,11},{13,12},{14,15},{17,16},{18,... | collective-permute-start | bytes 3145736 | tf_op jit(solution)/shard_map/ppermute | solution.py:199
  68.1 87.0 %copy-start.3 = (f32[512,128]{1,0:T(8,128)S(1)}, f32[512,128]{1,0:T(8,128)}, u32[]{:S(2)}) copy-start(f32[512,128]{1,0:T(8,128)} %coefficients.1) | copy-start | bytes 786436
  68.1 1.0 copy-start.1
  144.6 10.5 %collective-permute-start.7 = (f32[2048,128]{1,0:T(8,128)}, f32[2048,128]{1,0:T(8,128)}, u32[]{:S(2)}, u32[]{:S(2)}) collective-permute-start(f32[2048,128]{1,0:T(8,128)} %bitcast.12.own_packed), channel_id=1, source_target_pairs={{0,4},{4,0},{1,5},{5,1},{2,6},{6,2},{3,7},{7,3},{8,12},{12,8},{9,1... | collective-permute-start | bytes 3145736 | tf_op jit(solution)/shard_map/ppermute | solution.py:224
  152.6 27.8 %copy-start.2 = (f32[2048,128]{1,0:T(8,128)S(1)}, f32[2048,128]{1,0:T(8,128)}, u32[]{:S(2)}) copy-start(f32[2048,128]{1,0:T(8,128)} %copy-done.1) | copy-start | bytes 3145732

commit v3 on v2

--- a/solution.py
+++ b/solution.py
@@ -193,8 +193,8 @@
 
     pairs = send(x_block, perm=[(0, 1), (1, 0), (2, 3), (3, 2)])
     middle = send(x_block, perm=[(1, 2), (2, 1)])
+    outer_h = send(h_block, perm=[(0, 1), (3, 2)])
     across = send(pairs, perm=[(1, 2), (2, 1)])
-    outer_h = send(after(h_block, pairs), perm=[(0, 1), (3, 2)])
     outward = send(middle, perm=[(1, 0), (2, 3)])
     far = send(across, perm=[(1, 0), (2, 3)])
     times = functools.partial(
@@ -204,14 +204,9 @@
         preferred_element_type=jnp.float32,
     )
     near = jnp.concatenate([x_block, pairs, middle], axis=1)
-    early = mass_weights[:, None] * jnp.concatenate([pairs, x_block, h_block], axis=1)
-    late = mass_weights[:, None] * outer_h
-    near_early, near_late = times(near, early), times(near, late)
-    far_early, far_late = times(across, early), times(across, late)
-    gram = jnp.concatenate([near_early[:, : 2 * width], far_early[:, : 2 * width]], axis=0)
-    hamil_outer = jnp.concatenate([near_late, far_late], axis=0)
-    hamil_own = jnp.concatenate([near_early[:, 2 * width :], far_early[:, 2 * width :]], axis=0)
-    hamil = jnp.concatenate([hamil_outer, hamil_own], axis=1)
+    weighted = mass_weights[:, None] * jnp.concatenate([pairs, x_block, outer_h, h_block], axis=1)
+    products = jnp.concatenate([times(near, weighted), times(across, weighted)], axis=0)
+    gram, hamil = products[:, : 2 * width], products[:, 2 * width :]
 
     kept, sent = jnp.where(core == 0, gram, hamil), jnp.where(core == 0, hamil, gram)
     summed = kept + lax.ppermute(sent, "core", [(0, 1), (1, 0)])

time: 186 us -> 179 us (0.962)
  matrix products: 11.6 us -> 8.6 us
  local copies, waits for them, and re-layouts: 3.43 us -> 1.21 us
  blocking collectives: 72.9 us -> 74.9 us
    ppermute x1, waiting for transfers between devices: 17.8 us -> 11.2 us  [shards(): pairs = send(x_block, perm=[(0, 1), (1, 0), (2, 3), (3, 2)])]
    ppermute x1, waiting for transfers between devices: 13.1 us -> 19.3 us  [shards(): outer_h = send(h_block, perm=[(0, 1), (3, 2)])]
    dot_general x4 -> x2, matrix products: 11.6 us -> 8.6 us  [the longest x1 5.48 us: shards(): times(near, weighted)]
    ppermute x1, starting transfers between devices: 4.65 us -> 7.14 us  [shards(): summed = kept + lax.ppermute(sent, 'core', [(0, 1), (1, 0)])]
    ppermute x1, starting transfers between devices: 9.15 us -> 6.69 us  [shards(): outer_h = send(h_block, perm=[(0, 1), (3, 2)])]
    all_to_all x3, blocking collectives: 72.9 us -> 74.9 us  [exchange(): return lax.all_to_all(value, axes, 0, 0, tiled=True)]
  transfers between devices with their start and end apart: 8 -> 8, of which waited for: 4 -> 4; matrix products, arithmetic and copies ran while one was open for 8% -> 5% of each run, Pallas kernels for 0% -> 0%
where the time goes in v3:
time: 179 us
  blocking collectives  74.9 us (42%)
  waiting for transfers between devices  32.9 us (18%)
  starting transfers between devices  30.4 us (17%)
  Pallas kernels  29.5 us (16%)
  matrix products  8.6 us (5%)
    all_to_all x3, blocking collectives, exchange(): return lax.all_to_all(value, axes, 0, 0, tiled=True)  74.9 us
    pallas_call x1, Pallas kernels, solve(): pl.pallas_call(small_matrices, out_shape=(result, result), in_specs=[pl.B...  25 us
    ppermute x1, waiting for transfers between devices, shards(): outer_h = send(h_block, perm=[(0, 1), (3, 2)])  19.3 us
    ppermute x1, waiting for transfers between devices, shards(): pairs = send(x_block, perm=[(0, 1), (1, 0), (2, 3), (3, 2)])  11.2 us
    ppermute x1, starting transfers between devices, shards(): other = lax.ppermute(summed, 'core', [(0, 1), (1, 0)])  7.33 us
    ppermute x1, starting transfers between devices, shards(): summed = kept + lax.ppermute(sent, 'core', [(0, 1), (1, 0)])  7.14 us
    ppermute x1, starting transfers between devices, shards(): outer_h = send(h_block, perm=[(0, 1), (3, 2)])  6.69 us
    dot_general x1, matrix products, shards(): times(near, weighted)  5.48 us
  transfers between devices with their start and end apart: 8, of which 4 were waited for; matrix products, arithmetic and copies ran while one was open for 5% of the time, Pallas kernels for 0%

profile of v3, /device:TPU:1, one launch (start us, length us, event | category | flops | bytes accessed | tf_op | source)
XLA Modules:
  0.0 178.6 jit_solution(5821358534107494268)
XLA Ops:
  0.6 4.0 %collective-permute-start = (f32[2048,128]{1,0:T(8,128)}, f32[2048,128]{1,0:T(8,128)S(1)}, u32[]{:S(2)}, u32[]{:S(2)}) collective-permute-start(f32[2048,128]{1,0:T(8,128)} %own.1), channel_id=1, source_target_pairs={{0,1},{1,0},{2,3},{3,2},{4,5},{5,4},{6,7},{7,6},{8,9},{9,8},{10,11... | collective-permute-start | bytes 3145736 | tf_op jit(solution)/shard_map/ppermute | solution.py:194
  4.7 0.7 collective-permute-start.1
  5.4 6.7 %collective-permute-start.2 = (f32[2048,128]{1,0:T(8,128)}, f32[2048,128]{1,0:T(8,128)}, u32[]{:S(2)}, u32[]{:S(2)}) collective-permute-start(f32[2048,128]{1,0:T(8,128)} %param.5), channel_id=1, source_target_pairs={{0,1},{3,2},{4,5},{7,6},{8,9},{11,10},{12,13},{15,14},{16,17},{19,... | collective-permute-start | bytes 3145736 | tf_op jit(solution)/shard_map/ppermute | solution.py:196
  12.1 11.2 %collective-permute-done.pairs = f32[2048,128]{1,0:T(8,128)S(1)} collective-permute-done((f32[2048,128]{1,0:T(8,128)}, f32[2048,128]{1,0:T(8,128)S(1)}, u32[]{:S(2)}, u32[]{:S(2)}) %collective-permute-start) | collective-permute-done | bytes 1048608 | tf_op jit(solution)/shard_map/ppermute | solution.py:194
  23.3 1.6 collective-permute-start.3
  24.9 0.0 copy-start
  24.9 0.0 copy-start.6
  24.9 0.0 copy-start.7
  24.9 0.0 collective-permute-done.1.middle
  24.9 0.0 copy-start.1
  24.9 1.6 collective-permute-start.5
  26.5 19.3 %collective-permute-done.2 = f32[2048,128]{1,0:T(8,128)} collective-permute-done((f32[2048,128]{1,0:T(8,128)}, f32[2048,128]{1,0:T(8,128)}, u32[]{:S(2)}, u32[]{:S(2)}) %collective-permute-start.2) | collective-permute-done | bytes 1048608 | tf_op jit(solution)/shard_map/ppermute | solution.py:196
  45.8 5.5 %fusion = f32[384,512]{1,0:T(8,128)S(1)} fusion(f32[2048,128]{1,0:T(8,128)S(1)} %collective-permute-done.1.middle, f32[2048,128]{1,0:T(8,128)S(1)} %collective-permute-done.pairs, f32[2048,128]{1,0:T(8,128)} %own.1, f32[2048,128]{1,0:T(8,128)} %param.5, f32[2048,128]{1,0:T(8,128)} %collective-permute-done.2, f32[2048]{0:T(1024)} %param.6), kind=kOutput, calls=%fused_computation.1 | convolution fusion | flops 2421686272 | bytes 6037504 | tf_op jit(solution)/shard_map/dot_general | solution.py:208
  51.2 0.0 copy-done.1
  51.2 0.0 collective-permute-done.3.across
  51.3 0.0 copy-done
  51.3 0.0 copy-done.6
  51.3 0.0 copy-done.7
  51.3 3.1 %fusion.9 = f32[128,512]{1,0:T(8,128)S(1)} fusion(f32[2048,128]{1,0:T(8,128)} %collective-permute-done.3.across, f32[2048,128]{1,0:T(8,128)S(1)} %copy-done.6, f32[2048,128]{1,0:T(8,128)} %collective-permute-done.2, f32[2048,128]{1,0:T(8,128)S(1)} %copy-done, f32[2048,128]{1,0:T(8,128)S(1)} %collective-permute-done.pairs, f32[2048]{0:T(1024)S(1)} %copy-done.7), kind=kOutput, calls=%fused_computation.10 | convolution fusion | flops 809500672 | bytes 5513216 | tf_op jit(solution)/shard_map/dot_general | solution.py:208
  54.4 0.1 broadcast_select_fusion
  54.5 7.1 %collective-permute-start.4 = (f32[512,256]{1,0:T(8,128)S(1)}, f32[512,256]{1,0:T(8,128)S(1)}, u32[]{:S(2)}, u32[]{:S(2)}) collective-permute-start(f32[512,256]{1,0:T(8,128)S(1)} %broadcast_select_fusion), channel_id=1, source_target_pairs={{0,4},{4,0},{1,5},{5,1},{2,6},{6,2},{3,7},{7,3},{8,12},{12,8},{9,1... | collective-permute-start | bytes 1572872 | tf_op jit(solution)/shard_map/ppermute | solution.py:212
  61.6 1.3 collective-permute-start.6
  62.9 0.2 collective-permute-done.4
  63.2 0.1 select_add_fusion
  63.3 0.0 collective-permute-done.5.outward
  63.3 0.0 copy-start.3
  63.3 1.0 copy-done.3
  64.3 26.6 %all_to_all.23 = f32[32,16,256]{2,1,0:T(8,128)S(1)} all-to-all(f32[32,16,256]{2,1,0:T(8,128)S(1)} %bitcast.18), channel_id=1, replica_groups=mesh['x'=4,'z'=8,'yh'=2,'core'=2,'state'=4] {'x','z'}, dimensions={0} | all-to-all | bytes 1048576 | tf_op jit(solution)/shard_map/all_to_all | solution.py:26
  91.0 0.0 collective-permute-done.6.far
  91.0 16.2 %all_to_all.24 = f32[8,16,256]{2,1,0:T(8,128)S(1)} all-to-all(f32[8,16,256]{2,1,0:T(8,128)S(1)} %broadcast_in_dim.7), channel_id=1, replica_groups=mesh['x'=4,'z'=8,'yh'=2,'core'=2,'state'=4] {'yh','state'}, dimensions={0} | all-to-all | bytes 262144 | tf_op jit(solution)/shard_map/all_to_all | solution.py:26
  107.2 0.1 broadcast_in_dim.8
  107.4 0.0 copy-start.5
  107.4 32.0 %all_to_all.25 = f32[32,64,128]{2,1,0:T(8,128)S(1)} all-to-all(f32[32,64,128]{2,1,0:T(8,128)S(1)} %broadcast_in_dim.8), channel_id=1, replica_groups=mesh['x'=4,'z'=8,'yh'=2,'core'=2,'state'=4] {'x','z'}, dimensions={0} | all-to-all | bytes 2097152 | tf_op jit(solution)/shard_map/all_to_all | solution.py:26
  139.4 7.3 %collective-permute-start.7 = (f32[2048,128]{1,0:T(8,128)S(1)}, f32[2048,128]{1,0:T(8,128)}, u32[]{:S(2)}, u32[]{:S(2)}) collective-permute-start(f32[2048,128]{1,0:T(8,128)S(1)} %bitcast.16), channel_id=1, source_target_pairs={{0,4},{4,0},{1,5},{5,1},{2,6},{6,2},{3,7},{7,3},{8,12},{12,8},{9,1... | collective-permute-start | bytes 3145736 | tf_op jit(solution)/shard_map/ppermute | solution.py:219
  146.8 0.1 stack.34.source_ref
  146.9 0.1 pad_add_fusion.place_ref
  146.9 0.0 copy-start.2
  146.9 0.0 copy-start.4
  146.9 2.2 %collective-permute-done.7.other_packed = f32[2048,128]{1,0:T(8,128)} collective-permute-done((f32[2048,128]{1,0:T(8,128)S(1)}, f32[2048,128]{1,0:T(8,128)}, u32[]{:S(2)}, u32[]{:S(2)}) %collective-permute-start.7) | collective-permute-done | bytes 1048608 | tf_op jit(solution)/shard_map/ppermute | solution.py:219
  149.1 0.0 copy-done.5
  149.1 25.0 %shard_map.59 = (f32[512,128]{1,0:T(8,128)S(1)}, f32[512,128]{1,0:T(8,128)}) custom-call(s32[2]{0:T(128)S(1)} %pad_add_fusion.place_ref, f32[2048,128]{1,0:T(8,128)S(1)} %bitcast.17, f32[2048,128]{1,0:T(8,128)} %collective-permute-done.7.other_packed, f32[512,128]{1,0:T(8,128)S(1)} %copy-done.5), custom_call_target="tpu_custom_call" | custom-call | flops 20000000000 | bytes 4194304 | tf_op jit(solution)/shard_map/pallas_call | solution.py:135
  174.2 0.0 copy-done.2
  174.2 0.0 copy-done.4
  174.2 4.4 %shard_map.60 = f32[2048,128]{1,0:T(8,128)} custom-call(s32[5]{0:T(128)S(1)} %stack.34.source_ref, f32[512,128]{1,0:T(8,128)S(1)} %get-tuple-element.8.rotation_ref, f32[2048,128]{1,0:T(8,128)S(1)} %copy-done, f32[2048,128]{1,0:T(8,128)S(1)} %collective-permute-done.pairs, f32[2048,128]{1,0:T(8,128)S(1)} %copy-done.2, f32[2048,128]{1,0:T(8,128)S(1)} %copy-done.4, ...), custom_call_target="tpu_custom_call" | custom-call | flops 2000000000 | bytes 8388608 | tf_op jit(solution)/shard_map/pallas_call | solution.py:174
  (6 shorter events, 0.1 us)
Async XLA Ops:
  0.6 22.7 %collective-permute-start = (f32[2048,128]{1,0:T(8,128)}, f32[2048,128]{1,0:T(8,128)S(1)}, u32[]{:S(2)}, u32[]{:S(2)}) collective-permute-start(f32[2048,128]{1,0:T(8,128)} %own.1), channel_id=1, source_target_pairs={{0,1},{1,0},{2,3},{3,2},{4,5},{5,4},{6,7},{7,6},{8,9},{9,8},{10,11... | collective-permute-start | bytes 3145736 | tf_op jit(solution)/shard_map/ppermute | solution.py:194
  4.7 20.2 %collective-permute-start.1 = (f32[2048,128]{1,0:T(8,128)}, f32[2048,128]{1,0:T(8,128)S(1)}, u32[]{:S(2)}, u32[]{:S(2)}) collective-permute-start(f32[2048,128]{1,0:T(8,128)} %own.1), channel_id=1, source_target_pairs={{1,2},{2,1},{5,6},{6,5},{9,10},{10,9},{13,14},{14,13},{17,18},{18,... | collective-permute-start | bytes 3145736 | tf_op jit(solution)/shard_map/ppermute | solution.py:195
  5.4 40.3 %collective-permute-start.2 = (f32[2048,128]{1,0:T(8,128)}, f32[2048,128]{1,0:T(8,128)}, u32[]{:S(2)}, u32[]{:S(2)}) collective-permute-start(f32[2048,128]{1,0:T(8,128)} %param.5), channel_id=1, source_target_pairs={{0,1},{3,2},{4,5},{7,6},{8,9},{11,10},{12,13},{15,14},{16,17},{19,... | collective-permute-start | bytes 3145736 | tf_op jit(solution)/shard_map/ppermute | solution.py:196
  23.3 28.0 %collective-permute-start.3 = (f32[2048,128]{1,0:T(8,128)S(1)}, f32[2048,128]{1,0:T(8,128)}, u32[]{:S(2)}, u32[]{:S(2)}) collective-permute-start(f32[2048,128]{1,0:T(8,128)S(1)} %collective-permute-done.pairs), channel_id=1, source_target_pairs={{1,2},{2,1},{5,6},{6,5},{9,10},{10,9},{13,14},{14,13},{17,18},{18,... | collective-permute-start | bytes 3145736 | tf_op jit(solution)/shard_map/ppermute | solution.py:197
  24.9 26.4 %copy-start = (f32[2048,128]{1,0:T(8,128)S(1)}, f32[2048,128]{1,0:T(8,128)}, u32[]{:S(2)}) copy-start(f32[2048,128]{1,0:T(8,128)} %own.1) | copy-start | bytes 3145732
  24.9 26.4 %copy-start.6 = (f32[2048,128]{1,0:T(8,128)S(1)}, f32[2048,128]{1,0:T(8,128)}, u32[]{:S(2)}) copy-start(f32[2048,128]{1,0:T(8,128)} %param.5) | copy-start | bytes 3145732
  24.9 26.4 %copy-start.7 = (f32[2048]{0:T(1024)S(1)}, f32[2048]{0:T(1024)}, u32[]{:S(2)}) copy-start(f32[2048]{0:T(1024)} %param.6) | copy-start | bytes 24580
  24.9 26.3 %copy-start.1 = (f32[2048,128]{1,0:T(8,128)}, f32[2048,128]{1,0:T(8,128)S(1)}, u32[]{:S(2)}) copy-start(f32[2048,128]{1,0:T(8,128)S(1)} %collective-permute-done.1.middle) | copy-start | bytes 3145732
  24.9 38.4 %collective-permute-start.5 = (f32[2048,128]{1,0:T(8,128)S(1)}, f32[2048,128]{1,0:T(8,128)S(1)}, u32[]{:S(2)}, u32[]{:S(2)}) collective-permute-start(f32[2048,128]{1,0:T(8,128)S(1)} %collective-permute-done.1.middle), channel_id=1, source_target_pairs={{1,0},{2,3},{5,4},{6,7},{9,8},{10,11},{13,12},{14,15},{17,16},{18,... | collective-permute-start | bytes 3145736 | tf_op jit(solution)/shard_map/ppermute | solution.py:198
  54.5 8.7 %collective-permute-start.4 = (f32[512,256]{1,0:T(8,128)S(1)}, f32[512,256]{1,0:T(8,128)S(1)}, u32[]{:S(2)}, u32[]{:S(2)}) collective-permute-start(f32[512,256]{1,0:T(8,128)S(1)} %broadcast_select_fusion), channel_id=1, source_target_pairs={{0,4},{4,0},{1,5},{5,1},{2,6},{6,2},{3,7},{7,3},{8,12},{12,8},{9,1... | collective-permute-start | bytes 1572872 | tf_op jit(solution)/shard_map/ppermute | solution.py:212
  61.6 29.3 %collective-permute-start.6 = (f32[2048,128]{1,0:T(8,128)}, f32[2048,128]{1,0:T(8,128)}, u32[]{:S(2)}, u32[]{:S(2)}) collective-permute-start(f32[2048,128]{1,0:T(8,128)} %collective-permute-done.3.across), channel_id=1, source_target_pairs={{1,0},{2,3},{5,4},{6,7},{9,8},{10,11},{13,12},{14,15},{17,16},{18,... | collective-permute-start | bytes 3145736 | tf_op jit(solution)/shard_map/ppermute | solution.py:199
  63.3 1.0 copy-start.3
  107.4 41.8 %copy-start.5 = (f32[512,128]{1,0:T(8,128)S(1)}, f32[512,128]{1,0:T(8,128)}, u32[]{:S(2)}) copy-start(f32[512,128]{1,0:T(8,128)} %coefficients.1) | copy-start | bytes 786436
  139.4 9.7 %collective-permute-start.7 = (f32[2048,128]{1,0:T(8,128)S(1)}, f32[2048,128]{1,0:T(8,128)}, u32[]{:S(2)}, u32[]{:S(2)}) collective-permute-start(f32[2048,128]{1,0:T(8,128)S(1)} %bitcast.16), channel_id=1, source_target_pairs={{0,4},{4,0},{1,5},{5,1},{2,6},{6,2},{3,7},{7,3},{8,12},{12,8},{9,1... | collective-permute-start | bytes 3145736 | tf_op jit(solution)/shard_map/ppermute | solution.py:219
  146.9 27.3 %copy-start.2 = (f32[2048,128]{1,0:T(8,128)S(1)}, f32[2048,128]{1,0:T(8,128)}, u32[]{:S(2)}) copy-start(f32[2048,128]{1,0:T(8,128)} %copy-done.1) | copy-start | bytes 3145732
  146.9 27.3 %copy-start.4 = (f32[2048,128]{1,0:T(8,128)S(1)}, f32[2048,128]{1,0:T(8,128)}, u32[]{:S(2)}) copy-start(f32[2048,128]{1,0:T(8,128)} %copy-done.3) | copy-start | bytes 3145732

commit v4 on v3

--- a/solution.py
+++ b/solution.py
@@ -204,19 +204,25 @@
         preferred_element_type=jnp.float32,
     )
     near = jnp.concatenate([x_block, pairs, middle], axis=1)
-    weighted = mass_weights[:, None] * jnp.concatenate([pairs, x_block, outer_h, h_block], axis=1)
-    products = jnp.concatenate([times(near, weighted), times(across, weighted)], axis=0)
-    gram, hamil = products[:, : 2 * width], products[:, 2 * width :]
+    early = mass_weights[:, None] * jnp.concatenate([pairs, x_block, h_block], axis=1)
+    near_early = times(near, early)
+    outer_h, last = after((outer_h, across), near_early)
+    late = mass_weights[:, None] * outer_h
+    near_late = times(near, late)
+    far_all = times(last, jnp.concatenate([early, late], axis=1))
+    gram = jnp.concatenate([near_early[:, : 2 * width], far_all[:, : 2 * width]], axis=0)
+    hamil_outer = jnp.concatenate([near_late, far_all[:, 3 * width :]], axis=0)
+    hamil_own = jnp.concatenate([near_early[:, 2 * width :], far_all[:, 2 * width : 3 * width]], axis=0)
+    hamil = jnp.concatenate([hamil_outer, hamil_own], axis=1)
 
     kept, sent = jnp.where(core == 0, gram, hamil), jnp.where(core == 0, hamil, gram)
     summed = kept + lax.ppermute(sent, "core", [(0, 1), (1, 0)])
     summed = total(exchange(after(summed, outward), PLANE), PLANE)
-    summed = after(summed, far)
     shape = (lax.axis_size("yh"), lax.axis_size("state")) + summed.shape
     summed = jnp.sum(exchange(copies(summed, LINE), LINE).reshape(shape), axis=0)
     panels = summed[1][:, :width], summed[1][:, width:], summed[2][:, width:], summed[2][:, :width]
     summed = exchange(copies(jnp.concatenate(panels, axis=0), PLANE), PLANE)
-    other = lax.ppermute(summed, "core", [(0, 1), (1, 0)])
+    other = lax.ppermute(after(summed, far), "core", [(0, 1), (1, 0)])
     rotation, projected = solve(jnp.stack([core, state]), summed, other, coefficients)
     rotated = rotate(state, rotation, x_block, pairs, middle, outward, across, far)
     return (rotated, projected)

time: 179 us -> 182 us (1.017)
  blocking collectives: 74.9 us -> 44.7 us
  waiting for transfers between devices: 32.9 us -> 53.6 us
  starting transfers between devices: 30.4 us -> 36.4 us
  local copies, waits for them, and re-layouts: 1.21 us -> 5.57 us
  other arithmetic: 0.35 us -> 4.26 us
    all_to_all x3 -> x2, blocking collectives: 74.9 us -> 44.7 us  [exchange(): return lax.all_to_all(value, axes, 0, 0, tiled=True)]
    ppermute x1, waiting for transfers between devices: 0.01 us -> 22.8 us  [shards(): far = send(across, perm=[(1, 0), (2, 3)])]
    all_to_all x0 -> x1, starting transfers between devices: none -> 8.09 us  [exchange(): return lax.all_to_all(value, axes, 0, 0, tiled=True)]
    unnamed x16 -> x22, local copies, waits for them, and re-layouts: 0.99 us -> 3.51 us
    mul x0 -> x2, other arithmetic: none -> 2.27 us  [the longest x1 1.93 us: shards(): late = mass_weights[:, None] * outer_h]
    ppermute x1, waiting for transfers between devices: 19.3 us -> 17.1 us  [shards(): outer_h = send(h_block, perm=[(0, 1), (3, 2)])]
    dot_general x2 -> x3, matrix products: 8.6 us -> 7.02 us  [the longest x1 2.76 us: shards(): near_early = times(near, early)]
  transfers between devices with their start and end apart: 8 -> 9, of which waited for: 4 -> 5; matrix products, arithmetic and copies ran while one was open for 5% -> 6% of each run, Pallas kernels for 0% -> 0%
where the time goes in v4:
time: 182 us; the launch traced here: 181 us
  waiting for transfers between devices  53.6 us (29%)
  blocking collectives  44.7 us (25%)
  starting transfers between devices  36.4 us (20%)
  Pallas kernels  28.7 us (16%)
  matrix products  7.02 us (4%)
  local copies, waits for them, and re-layouts  5.57 us (3%)
  other arithmetic  4.26 us (2%)
    all_to_all x2, blocking collectives, exchange(): return lax.all_to_all(value, axes, 0, 0, tiled=True)  44.7 us
    pallas_call x1, Pallas kernels, solve(): pl.pallas_call(small_matrices, out_shape=(result, result), in_specs=[pl.B...  25.4 us
    ppermute x1, waiting for transfers between devices, shards(): far = send(across, perm=[(1, 0), (2, 3)])  22.8 us
    ppermute x1, waiting for transfers between devices, shards(): outer_h = send(h_block, perm=[(0, 1), (3, 2)])  17.1 us
    ppermute x1, waiting for transfers between devices, shards(): pairs = send(x_block, perm=[(0, 1), (1, 0), (2, 3), (3, 2)])  9.74 us
    all_to_all x1, starting transfers between devices, exchange(): return lax.all_to_all(value, axes, 0, 0, tiled=True)  8.09 us
    ppermute x1, starting transfers between devices, shards(): summed = kept + lax.ppermute(sent, 'core', [(0, 1), (1, 0)])  7.14 us
    ppermute x1, starting transfers between devices, shards(): outer_h = send(h_block, perm=[(0, 1), (3, 2)])  6.68 us
  transfers between devices with their start and end apart: 9, of which 5 were waited for; matrix products, arithmetic and copies ran while one was open for 6% of the time, Pallas kernels for 0%

profile of v4, /device:TPU:1, one launch (start us, length us, event | category | flops | bytes accessed | tf_op | source)
XLA Modules:
  0.0 181.1 jit_solution(18404077778426515401)
XLA Ops:
  0.6 4.0 %collective-permute-start = (f32[2048,128]{1,0:T(8,128)}, f32[2048,128]{1,0:T(8,128)S(1)}, u32[]{:S(2)}, u32[]{:S(2)}) collective-permute-start(f32[2048,128]{1,0:T(8,128)} %own.1), channel_id=1, source_target_pairs={{0,1},{1,0},{2,3},{3,2},{4,5},{5,4},{6,7},{7,6},{8,9},{9,8},{10,11... | collective-permute-start | bytes 3145736 | tf_op jit(solution)/shard_map/ppermute | solution.py:194
  4.7 0.7 collective-permute-start.1
  5.4 6.7 %collective-permute-start.2 = (f32[2048,128]{1,0:T(8,128)}, f32[2048,128]{1,0:T(8,128)}, u32[]{:S(2)}, u32[]{:S(2)}) collective-permute-start(f32[2048,128]{1,0:T(8,128)} %param.5), channel_id=1, source_target_pairs={{0,1},{3,2},{4,5},{7,6},{8,9},{11,10},{12,13},{15,14},{16,17},{19,... | collective-permute-start | bytes 3145736 | tf_op jit(solution)/shard_map/ppermute | solution.py:196
  12.1 1.4 constant_dynamic-update-slice_fusion.2
  13.5 9.7 %collective-permute-done.pairs = f32[2048,128]{1,0:T(8,128)S(1)} collective-permute-done((f32[2048,128]{1,0:T(8,128)}, f32[2048,128]{1,0:T(8,128)S(1)}, u32[]{:S(2)}, u32[]{:S(2)}) %collective-permute-start) | collective-permute-done | bytes 1048608 | tf_op jit(solution)/shard_map/ppermute | solution.py:194
  23.3 0.7 collective-permute-start.3
  24.0 0.1 constant_dynamic-update-slice_fusion.1
  24.1 0.0 collective-permute-done.1.middle
  24.1 0.1 constant_dynamic-update-slice_fusion
  24.2 0.0 copy-done
  24.2 0.0 copy-done.8
  24.2 0.0 copy-done.9
  24.2 0.3 maximum_multiply_fusion
  24.6 2.8 %fusion.9 = f32[384,384]{1,0:T(8,128)S(1)} fusion(f32[2048,384]{1,0:T(8,128)S(1)} %constant_dynamic-update-slice_fusion, f32[2048,384]{1,0:T(8,128)S(1)} %maximum_multiply_fusion), kind=kOutput, calls=%fused_computation.21 | convolution fusion | flops 1811939328 | bytes 6881280 | tf_op jit(solution)/shard_map/dot_general | solution.py:208
  27.4 1.3 collective-permute-start.5
  28.7 17.1 %collective-permute-done.2 = f32[2048,128]{1,0:T(8,128)} collective-permute-done((f32[2048,128]{1,0:T(8,128)}, f32[2048,128]{1,0:T(8,128)}, u32[]{:S(2)}, u32[]{:S(2)}) %collective-permute-start.2) | collective-permute-done | bytes 1048608 | tf_op jit(solution)/shard_map/ppermute | solution.py:196
  45.8 0.0 collective-permute-done.3.across
  45.8 1.9 %broadcast_multiply_fusion = f32[2048,128]{1,0:T(8,128)S(1)} fusion(f32[2048,128]{1,0:T(8,128)} %collective-permute-done.2, f32[2048]{0:T(1024)S(1)} %copy-done.9), kind=kLoop, calls=%fused_computation.8 | loop fusion | flops 262144 | bytes 2105344 | tf_op jit(solution)/shard_map/mul | solution.py:210
  47.7 2.7 %fusion.10 = f32[384,128]{1,0:T(8,128)S(1)} fusion(f32[2048,384]{1,0:T(8,128)S(1)} %constant_dynamic-update-slice_fusion, f32[2048,128]{1,0:T(8,128)S(1)} %broadcast_multiply_fusion), kind=kOutput, calls=%fused_computation.22 | convolution fusion | flops 603979776 | bytes 4390912 | tf_op jit(solution)/shard_map/dot_general | solution.py:211
  50.4 0.0 copy-done.1
  50.4 1.6 fusion
  52.0 0.1 fusion.4
  52.1 7.1 %collective-permute-start.4 = (f32[512,256]{1,0:T(8,128)S(1)}, f32[512,256]{1,0:T(8,128)S(1)}, u32[]{:S(2)}, u32[]{:S(2)}) collective-permute-start(f32[512,256]{1,0:T(8,128)S(1)} %fusion.4), channel_id=1, source_target_pairs={{0,4},{4,0},{1,5},{5,1},{2,6},{6,2},{3,7},{7,3},{8,12},{12,8},{9,1... | collective-permute-start | bytes 1572872 | tf_op jit(solution)/shard_map/ppermute | solution.py:219
  59.2 1.5 collective-permute-done.4
  60.7 0.1 select_add_fusion
  60.9 0.0 copy-start.7
  60.9 0.0 collective-permute-done.5.outward
  60.9 0.0 copy-start.3
  60.9 1.0 copy-done.3
  61.9 26.8 %all_to_all.23 = f32[32,16,256]{2,1,0:T(8,128)} all-to-all(f32[32,16,256]{2,1,0:T(8,128)S(1)} %bitcast.18), channel_id=1, replica_groups=mesh['x'=4,'z'=8,'yh'=2,'core'=2,'state'=4] {'x','z'}, dimensions={0} | all-to-all | bytes 1048576 | tf_op jit(solution)/shard_map/all_to_all | solution.py:26
  88.6 1.1 reduce_sum.18
  89.7 18.0 %all_to_all.24 = f32[8,16,256]{2,1,0:T(8,128)S(1)} all-to-all(f32[8,16,256]{2,1,0:T(8,128)S(1)} %broadcast_in_dim.8), channel_id=1, replica_groups=mesh['x'=4,'z'=8,'yh'=2,'core'=2,'state'=4] {'yh','state'}, dimensions={0} | all-to-all | bytes 262144 | tf_op jit(solution)/shard_map/all_to_all | solution.py:26
  107.7 0.6 reduce_sum.19
  108.4 0.7 slice_bitcast_fusion.1
  109.1 1.1 broadcast_in_dim.9
  110.2 8.1 %all-to-all-start.2 = ((f32[32,64,128]{2,1,0:T(8,128)}), f32[32,64,128]{2,1,0:T(8,128)}, u32[]{:S(2)}, u32[]{:S(2)}) async-start(f32[32,64,128]{2,1,0:T(8,128)} %broadcast_in_dim.9), calls=%async_computation.2 | async-start | bytes 2097152 | tf_op jit(solution)/shard_map/all_to_all | solution.py:26
  118.3 1.3 collective-permute-start.6
  119.6 22.8 %collective-permute-done.6.far = f32[2048,128]{1,0:T(8,128)S(1)} collective-permute-done((f32[2048,128]{1,0:T(8,128)}, f32[2048,128]{1,0:T(8,128)S(1)}, u32[]{:S(2)}, u32[]{:S(2)}) %collective-permute-start.6) | collective-permute-done | bytes 1048608 | tf_op jit(solution)/shard_map/ppermute | solution.py:199
  142.4 1.0 copy-done.5
  143.4 0.0 all-to-all-done.2
  143.4 6.4 %collective-permute-start.7 = (f32[2048,128]{1,0:T(8,128)}, f32[2048,128]{1,0:T(8,128)}, u32[]{:S(2)}, u32[]{:S(2)}) collective-permute-start(f32[2048,128]{1,0:T(8,128)} %bitcast.10.own_packed), channel_id=1, source_target_pairs={{0,4},{4,0},{1,5},{5,1},{2,6},{6,2},{3,7},{7,3},{8,12},{12,8},{9,1... | collective-permute-start | bytes 3145736 | tf_op jit(solution)/shard_map/ppermute | solution.py:225
  149.8 0.1 stack.34.source_ref
  149.9 0.1 pad_add_fusion.place_ref
  150.0 2.4 %collective-permute-done.7.other_packed = f32[2048,128]{1,0:T(8,128)} collective-permute-done((f32[2048,128]{1,0:T(8,128)}, f32[2048,128]{1,0:T(8,128)}, u32[]{:S(2)}, u32[]{:S(2)}) %collective-permute-start.7) | collective-permute-done | bytes 1048608 | tf_op jit(solution)/shard_map/ppermute | solution.py:225
  152.4 0.0 copy-done.7
  152.4 25.4 %shard_map.59 = (f32[512,128]{1,0:T(8,128)S(1)}, f32[512,128]{1,0:T(8,128)}) custom-call(s32[2]{0:T(128)S(1)} %pad_add_fusion.place_ref, f32[2048,128]{1,0:T(8,128)} %bitcast.10.own_packed, f32[2048,128]{1,0:T(8,128)} %collective-permute-done.7.other_packed, f32[512,128]{1,0:T(8,128)S(1)} %copy-done.7), custom_call_target="tpu_custom_call" | custom-call | flops 20000000000 | bytes 4194304 | tf_op jit(solution)/shard_map/pallas_call | solution.py:135
  177.8 0.0 copy-done.4
  177.8 3.3 %shard_map.60 = f32[2048,128]{1,0:T(8,128)} custom-call(s32[5]{0:T(128)S(1)} %stack.34.source_ref, f32[512,128]{1,0:T(8,128)S(1)} %get-tuple-element.12.rotation_ref, f32[2048,128]{1,0:T(8,128)S(1)} %copy-done, f32[2048,128]{1,0:T(8,128)S(1)} %collective-permute-done.pairs, f32[2048,128]{1,0:T(8,128)S(1)} %collective-permute-done.1.middle, ...), custom_call_target="tpu_custom_call" | custom-call | flops 2000000000 | bytes 8388608 | tf_op jit(solution)/shard_map/pallas_call | solution.py:174
  (17 shorter events, 0.1 us)
Async XLA Ops:
  0.6 22.7 %collective-permute-start = (f32[2048,128]{1,0:T(8,128)}, f32[2048,128]{1,0:T(8,128)S(1)}, u32[]{:S(2)}, u32[]{:S(2)}) collective-permute-start(f32[2048,128]{1,0:T(8,128)} %own.1), channel_id=1, source_target_pairs={{0,1},{1,0},{2,3},{3,2},{4,5},{5,4},{6,7},{7,6},{8,9},{9,8},{10,11... | collective-permute-start | bytes 3145736 | tf_op jit(solution)/shard_map/ppermute | solution.py:194
  4.7 19.4 %collective-permute-start.1 = (f32[2048,128]{1,0:T(8,128)}, f32[2048,128]{1,0:T(8,128)S(1)}, u32[]{:S(2)}, u32[]{:S(2)}) collective-permute-start(f32[2048,128]{1,0:T(8,128)} %own.1), channel_id=1, source_target_pairs={{1,2},{2,1},{5,6},{6,5},{9,10},{10,9},{13,14},{14,13},{17,18},{18,... | collective-permute-start | bytes 3145736 | tf_op jit(solution)/shard_map/ppermute | solution.py:195
  5.4 40.3 %collective-permute-start.2 = (f32[2048,128]{1,0:T(8,128)}, f32[2048,128]{1,0:T(8,128)}, u32[]{:S(2)}, u32[]{:S(2)}) collective-permute-start(f32[2048,128]{1,0:T(8,128)} %param.5), channel_id=1, source_target_pairs={{0,1},{3,2},{4,5},{7,6},{8,9},{11,10},{12,13},{15,14},{16,17},{19,... | collective-permute-start | bytes 3145736 | tf_op jit(solution)/shard_map/ppermute | solution.py:196
  12.1 12.1 %copy-start = (f32[2048,128]{1,0:T(8,128)S(1)}, f32[2048,128]{1,0:T(8,128)}, u32[]{:S(2)}) copy-start(f32[2048,128]{1,0:T(8,128)} %own.1) | copy-start | bytes 3145732
  12.1 12.1 %copy-start.8 = (f32[2048,128]{1,0:T(8,128)S(1)}, f32[2048,128]{1,0:T(8,128)}, u32[]{:S(2)}) copy-start(f32[2048,128]{1,0:T(8,128)} %param.5) | copy-start | bytes 3145732
  12.1 12.1 %copy-start.9 = (f32[2048]{0:T(1024)S(1)}, f32[2048]{0:T(1024)}, u32[]{:S(2)}) copy-start(f32[2048]{0:T(1024)} %param.6) | copy-start | bytes 24580
  23.3 22.5 %collective-permute-start.3 = (f32[2048,128]{1,0:T(8,128)S(1)}, f32[2048,128]{1,0:T(8,128)S(1)}, u32[]{:S(2)}, u32[]{:S(2)}) collective-permute-start(f32[2048,128]{1,0:T(8,128)S(1)} %collective-permute-done.pairs), channel_id=1, source_target_pairs={{1,2},{2,1},{5,6},{6,5},{9,10},{10,9},{13,14},{14,13},{17,18},{18,... | collective-permute-start | bytes 3145736 | tf_op jit(solution)/shard_map/ppermute | solution.py:197
  27.4 33.5 %collective-permute-start.5 = (f32[2048,128]{1,0:T(8,128)S(1)}, f32[2048,128]{1,0:T(8,128)S(1)}, u32[]{:S(2)}, u32[]{:S(2)}) collective-permute-start(f32[2048,128]{1,0:T(8,128)S(1)} %collective-permute-done.1.middle), channel_id=1, source_target_pairs={{1,0},{2,3},{5,4},{6,7},{9,8},{10,11},{13,12},{14,15},{17,16},{18,... | collective-permute-start | bytes 3145736 | tf_op jit(solution)/shard_map/ppermute | solution.py:198
  45.8 4.6 %copy-start.1 = (f32[2048,128]{1,0:T(8,128)}, f32[2048,128]{1,0:T(8,128)S(1)}, u32[]{:S(2)}) copy-start(f32[2048,128]{1,0:T(8,128)S(1)} %collective-permute-done.3.across) | copy-start | bytes 3145732
  52.1 8.7 %collective-permute-start.4 = (f32[512,256]{1,0:T(8,128)S(1)}, f32[512,256]{1,0:T(8,128)S(1)}, u32[]{:S(2)}, u32[]{:S(2)}) collective-permute-start(f32[512,256]{1,0:T(8,128)S(1)} %fusion.4), channel_id=1, source_target_pairs={{0,4},{4,0},{1,5},{5,1},{2,6},{6,2},{3,7},{7,3},{8,12},{12,8},{9,1... | collective-permute-start | bytes 1572872 | tf_op jit(solution)/shard_map/ppermute | solution.py:219
  60.9 91.5 %copy-start.7 = (f32[512,128]{1,0:T(8,128)S(1)}, f32[512,128]{1,0:T(8,128)}, u32[]{:S(2)}) copy-start(f32[512,128]{1,0:T(8,128)} %coefficients.1) | copy-start | bytes 786436
  60.9 1.0 copy-start.3
  110.2 33.2 %all-to-all-start.2 = ((f32[32,64,128]{2,1,0:T(8,128)}), f32[32,64,128]{2,1,0:T(8,128)}, u32[]{:S(2)}, u32[]{:S(2)}) async-start(f32[32,64,128]{2,1,0:T(8,128)} %broadcast_in_dim.9), calls=%async_computation.2 | async-start | bytes 2097152 | tf_op jit(solution)/shard_map/all_to_all | solution.py:26
  118.3 24.1 %collective-permute-start.6 = (f32[2048,128]{1,0:T(8,128)}, f32[2048,128]{1,0:T(8,128)S(1)}, u32[]{:S(2)}, u32[]{:S(2)}) collective-permute-start(f32[2048,128]{1,0:T(8,128)} %copy-done.1), channel_id=1, source_target_pairs={{1,0},{2,3},{5,4},{6,7},{9,8},{10,11},{13,12},{14,15},{17,16},{18,... | collective-permute-start | bytes 3145736 | tf_op jit(solution)/shard_map/ppermute | solution.py:199
  142.4 1.0 copy-start.5
  143.4 9.0 %collective-permute-start.7 = (f32[2048,128]{1,0:T(8,128)}, f32[2048,128]{1,0:T(8,128)}, u32[]{:S(2)}, u32[]{:S(2)}) collective-permute-start(f32[2048,128]{1,0:T(8,128)} %bitcast.10.own_packed), channel_id=1, source_target_pairs={{0,4},{4,0},{1,5},{5,1},{2,6},{6,2},{3,7},{7,3},{8,12},{12,8},{9,1... | collective-permute-start | bytes 3145736 | tf_op jit(solution)/shard_map/ppermute | solution.py:225
  150.0 27.8 %copy-start.2 = (f32[2048,128]{1,0:T(8,128)S(1)}, f32[2048,128]{1,0:T(8,128)}, u32[]{:S(2)}) copy-start(f32[2048,128]{1,0:T(8,128)} %copy-done.1) | copy-start | bytes 3145732
  150.0 27.8 %copy-start.4 = (f32[2048,128]{1,0:T(8,128)S(1)}, f32[2048,128]{1,0:T(8,128)}, u32[]{:S(2)}) copy-start(f32[2048,128]{1,0:T(8,128)} %copy-done.3) | copy-start | bytes 3145732
  150.0 27.8 %copy-start.6 = (f32[2048,128]{1,0:T(8,128)S(1)}, f32[2048,128]{1,0:T(8,128)}, u32[]{:S(2)}) copy-start(f32[2048,128]{1,0:T(8,128)} %copy-done.5) | copy-start | bytes 3145732

commit v5 on v4

--- a/solution.py
+++ b/solution.py
@@ -69,29 +69,29 @@
     return right
 
 
-def unpack(packed, matrix):
-    panels = matrix.shape[1] // EDGE
-    for run in range(matrix.shape[0] // RUN):
-        for panel in range(panels):
-            at = (run * panels + panel) * RUN
-            first = ROW_ORDER[panel // 2][run * RUN // EDGE] * EDGE + run * RUN % EDGE
-            matrix[first : first + RUN, EDGE * panel : EDGE * (panel + 1)] = packed[at : at + RUN, :]
-
-
-def small_matrices(place_ref, own_packed, other_packed, coefficients, rotation_ref, projected_ref, work, hamil, inverse, block):
+def unpack(place_ref, own, other, matrix):
+    def place(arrays):
+        for run in range(matrix.shape[0] // RUN):
+            for panel in range(matrix.shape[1] // EDGE):
+                at = (2 * run + panel // 2) * RUN
+                first = ROW_ORDER[panel // 2][run * RUN // EDGE] * EDGE + run * RUN % EDGE
+                rows = arrays[panel in (1, 2)][at : at + RUN, :]
+                matrix[first : first + RUN, EDGE * panel : EDGE * (panel + 1)] = rows
+
+    @pl.when(place_ref[0] == 0)
+    def _():
+        place((own, other))
+
+    @pl.when(place_ref[0] != 0)
+    def _():
+        place((other, own))
+
+
+def factor_kernel(place_ref, own, other, coefficients, rotation_ref, inverse, work, block):
     nb = work.shape[0]
     blocks = nb // EDGE
     inverse[...] = jnp.zeros((nb, nb), jnp.float32)
-
-    @pl.when(place_ref[0] == 0)
-    def _():
-        unpack(own_packed, work)
-        unpack(other_packed, hamil)
-
-    @pl.when(place_ref[0] != 0)
-    def _():
-        unpack(other_packed, work)
-        unpack(own_packed, hamil)
+    unpack(place_ref, own, other, work)
 
     @pl.loop(0, blocks)
     def _(k):
@@ -120,27 +120,40 @@
     for j in range(blocks):
         low, high = EDGE * j, EDGE * (j + 1)
         rotation_ref[low:high, :] = dot(inverse[low:, low:high], coefficients[low:, :], BY_COLS)
-    own = pl.ds(pl.multiple_of(place_ref[1] * EDGE, EDGE), EDGE)
-    half = dot(hamil[...], inverse[own, :], BY_ROWS)
-    for j in range(blocks):
+
+def project_kernel(place_ref, own, other, inverse, projected_ref, hamil):
+    unpack(place_ref, own, other, hamil)
+    rows = pl.ds(pl.multiple_of(place_ref[1] * EDGE, EDGE), EDGE)
+    half = dot(hamil[...], inverse[rows, :], BY_ROWS)
+    for j in range(hamil.shape[0] // EDGE):
         high = EDGE * (j + 1)
         projected_ref[high - EDGE : high, :] = dot(inverse[high - EDGE : high, :high], half[:high], PLAIN)
 
 
-def solve(place, own_packed, other_packed, coefficients):
-    nb = coefficients.shape[0]
-    in_vmem = pl.BlockSpec(memory_space=pltpu.VMEM)
-    result = jax.ShapeDtypeStruct(coefficients.shape, jnp.float32)
-    square = pltpu.VMEM((nb, nb), jnp.float32)
+def in_vmem(kernel, out_shape, scratch_shapes, flops, place, *arrays):
+    spec = pl.BlockSpec(memory_space=pltpu.VMEM)
     return pl.pallas_call(
-        small_matrices,
-        out_shape=(result, result),
-        in_specs=[pl.BlockSpec(memory_space=pltpu.SMEM), in_vmem, in_vmem, in_vmem],
-        out_specs=(in_vmem, in_vmem),
-        scratch_shapes=[square, square, square, pltpu.VMEM((EDGE, EDGE), jnp.float32)],
-        cost_estimate=pl.CostEstimate(flops=2 * 10**10, bytes_accessed=2**22, transcendentals=0),
-        compiler_params=pltpu.CompilerParams(vmem_limit_bytes=32 * 2**20),
-    )(place, own_packed, other_packed, coefficients)
+        kernel,
+        out_shape=out_shape,
+        in_specs=[pl.BlockSpec(memory_space=pltpu.SMEM)] + [spec] * len(arrays),
+        out_specs=jax.tree.map(lambda _: spec, out_shape),
+        scratch_shapes=scratch_shapes,
+        cost_estimate=pl.CostEstimate(flops=flops, bytes_accessed=2**22, transcendentals=0),
+        compiler_params=pltpu.CompilerParams(vmem_limit_bytes=16 * 2**20),
+    )(place, *arrays)
+
+
+def factor(place, own, other, coefficients):
+    nb, width = coefficients.shape
+    outs = jax.ShapeDtypeStruct((nb, width), jnp.float32), jax.ShapeDtypeStruct((nb, nb), jnp.float32)
+    scratch = [pltpu.VMEM((nb, nb), jnp.float32), pltpu.VMEM((EDGE, EDGE), jnp.float32)]
+    return in_vmem(factor_kernel, outs, scratch, 2 * 10**10, place, own, other, coefficients)
+
+
+def project(place, own, other, inverse):
+    nb = inverse.shape[0]
+    out = jax.ShapeDtypeStruct((nb, EDGE), jnp.float32)
+    return in_vmem(project_kernel, out, [pltpu.VMEM((nb, nb), jnp.float32)], 10**9, place, own, other, inverse)
 
 
 def high_low(value):
@@ -182,7 +195,7 @@
         ],
         out_specs=by_rows,
         cost_estimate=pl.CostEstimate(flops=2 * 10**9, bytes_accessed=8 * 2**20, transcendentals=0),
-        compiler_params=pltpu.CompilerParams(vmem_limit_bytes=32 * 2**20),
+        compiler_params=pltpu.CompilerParams(vmem_limit_bytes=16 * 2**20),
     )(jnp.stack(sources), rotation, *blocks)
 
 
@@ -215,16 +228,22 @@
     hamil_own = jnp.concatenate([near_early[:, 2 * width :], far_all[:, 2 * width : 3 * width]], axis=0)
     hamil = jnp.concatenate([hamil_outer, hamil_own], axis=1)
 
-    kept, sent = jnp.where(core == 0, gram, hamil), jnp.where(core == 0, hamil, gram)
-    summed = kept + lax.ppermute(sent, "core", [(0, 1), (1, 0)])
+    outer = jnp.concatenate([gram[:, :width], hamil[:, :width]], axis=1)
+    inner = jnp.concatenate([gram[:, width:], hamil[:, width:]], axis=1)
+    kept, sent = jnp.where(core == 0, outer, inner), jnp.where(core == 0, inner, outer)
+    swap = functools.partial(lax.ppermute, axis_name="core", perm=[(0, 1), (1, 0)])
+    summed = kept + swap(sent)
     summed = total(exchange(after(summed, outward), PLANE), PLANE)
     shape = (lax.axis_size("yh"), lax.axis_size("state")) + summed.shape
-    summed = jnp.sum(exchange(copies(summed, LINE), LINE).reshape(shape), axis=0)
-    panels = summed[1][:, :width], summed[1][:, width:], summed[2][:, width:], summed[2][:, :width]
-    summed = exchange(copies(jnp.concatenate(panels, axis=0), PLANE), PLANE)
-    other = lax.ppermute(after(summed, far), "core", [(0, 1), (1, 0)])
-    rotation, projected = solve(jnp.stack([core, state]), summed, other, coefficients)
+    summed = jnp.sum(exchange(copies(summed, LINE), LINE).reshape(shape), axis=0)[1:3].reshape(-1, 2 * width)
+    gram, hamil = summed[:, :width], summed[:, width:]
+    gram = exchange(copies(gram, PLANE), PLANE)
+    hamil = exchange(copies(after(hamil, gram), PLANE), PLANE)
+    place = jnp.stack([core, state])
+    rotation, inverse = factor(place, gram, swap(gram), coefficients)
+    hamil = after(hamil, rotation)
     rotated = rotate(state, rotation, x_block, pairs, middle, outward, across, far)
+    projected = project(place, hamil, swap(hamil), inverse)
     return (rotated, projected)
 
 

time: 182 us -> 183 us (level)
  waiting for transfers between devices: 53.6 us -> 28.3 us
  blocking collectives: 44.7 us -> 65.1 us
  local copies, waits for them, and re-layouts: 5.57 us -> 8 us
  Pallas kernels: 28.7 us -> 30.6 us
    ppermute x1, waiting for transfers between devices: 22.8 us -> 0.01 us  [shards(): far = send(across, perm=[(1, 0), (2, 3)])]
    all_to_all x2 -> x3, blocking collectives: 44.7 us -> 65.1 us  [exchange(): return lax.all_to_all(value, axes, 0, 0, tiled=True)]
    unnamed x22, local copies, waits for them, and re-layouts: 3.51 us -> 6.86 us
    ppermute x2 -> x3, starting transfers between devices: 13.5 us -> 16.4 us  [the longest x1 7.14 us: shards(): summed = kept + swap(sent)]
    all_to_all x1, starting transfers between devices: 8.09 us -> 5.64 us  [exchange(): return lax.all_to_all(value, axes, 0, 0, tiled=True)]
    ppermute x2 -> x3, waiting for transfers between devices: 3.93 us -> 1.52 us  [the longest x1 1.51 us: shards(): summed = kept + swap(sent)]
    pallas_call x1 -> x2, Pallas kernels: 25.4 us -> 26.3 us  [in_vmem(): pl.pallas_call(kernel, out_shape=out_shape, in_specs=[pl.BlockSpec(memory...]
  transfers between devices with their start and end apart: 9 -> 10, of which waited for: 5 -> 3; matrix products, arithmetic and copies ran while one was open for 6% -> 7% of each run, Pallas kernels for 0% -> 14%
where the time goes in v5:
time: 183 us; the launch traced here: 180 us
  blocking collectives  65.1 us (36%)
  starting transfers between devices  36.7 us (20%)
  Pallas kernels  30.6 us (17%)
  waiting for transfers between devices  28.3 us (15%)
  local copies, waits for them, and re-layouts  8 us (4%)
  matrix products  7.02 us (4%)
  other arithmetic  3.65 us (2%)
    all_to_all x3, blocking collectives, exchange(): return lax.all_to_all(value, axes, 0, 0, tiled=True)  65.1 us
    pallas_call x2, Pallas kernels, in_vmem(): pl.pallas_call(kernel, out_shape=out_shape, in_specs=[pl.BlockSpec(memory...  26.3 us
    ppermute x1, waiting for transfers between devices, shards(): outer_h = send(h_block, perm=[(0, 1), (3, 2)])  17.1 us
    ppermute x1, waiting for transfers between devices, shards(): pairs = send(x_block, perm=[(0, 1), (1, 0), (2, 3), (3, 2)])  9.74 us
    ppermute x1, starting transfers between devices, shards(): summed = kept + swap(sent)  7.14 us
    ppermute x1, starting transfers between devices, shards(): rotation, inverse = factor(place, gram, swap(gram), coefficients)  7.03 us
    unnamed x22, local copies, waits for them, and re-layouts  6.86 us
    ppermute x1, starting transfers between devices, shards(): outer_h = send(h_block, perm=[(0, 1), (3, 2)])  6.68 us
  transfers between devices with their start and end apart: 10, of which 3 were waited for; matrix products, arithmetic and copies ran while one was open for 7% of the time, Pallas kernels for 14%

profile of v5, /device:TPU:1, one launch (start us, length us, event | category | flops | bytes accessed | tf_op | source)
XLA Modules:
  0.0 180.4 jit_solution(3419540099765376590)
XLA Ops:
  0.6 4.0 %collective-permute-start = (f32[2048,128]{1,0:T(8,128)}, f32[2048,128]{1,0:T(8,128)S(1)}, u32[]{:S(2)}, u32[]{:S(2)}) collective-permute-start(f32[2048,128]{1,0:T(8,128)} %own.1), channel_id=1, source_target_pairs={{0,1},{1,0},{2,3},{3,2},{4,5},{5,4},{6,7},{7,6},{8,9},{9,8},{10,11... | collective-permute-start | bytes 3145736 | tf_op jit(solution)/shard_map/ppermute | solution.py:207
  4.7 0.7 collective-permute-start.1
  5.4 6.7 %collective-permute-start.2 = (f32[2048,128]{1,0:T(8,128)}, f32[2048,128]{1,0:T(8,128)}, u32[]{:S(2)}, u32[]{:S(2)}) collective-permute-start(f32[2048,128]{1,0:T(8,128)} %param.5), channel_id=1, source_target_pairs={{0,1},{3,2},{4,5},{7,6},{8,9},{11,10},{12,13},{15,14},{16,17},{19,... | collective-permute-start | bytes 3145736 | tf_op jit(solution)/shard_map/ppermute | solution.py:209
  12.1 1.4 constant_dynamic-update-slice_fusion.2
  13.5 9.7 %collective-permute-done.pairs = f32[2048,128]{1,0:T(8,128)S(1)} collective-permute-done((f32[2048,128]{1,0:T(8,128)}, f32[2048,128]{1,0:T(8,128)S(1)}, u32[]{:S(2)}, u32[]{:S(2)}) %collective-permute-start) | collective-permute-done | bytes 1048608 | tf_op jit(solution)/shard_map/ppermute | solution.py:207
  23.3 0.7 collective-permute-start.3
  24.0 0.1 constant_dynamic-update-slice_fusion.1
  24.1 0.0 collective-permute-done.1.middle
  24.1 0.1 constant_dynamic-update-slice_fusion
  24.2 0.3 maximum_multiply_fusion
  24.6 2.8 %fusion.10 = f32[384,384]{1,0:T(8,128)S(1)} fusion(f32[2048,384]{1,0:T(8,128)S(1)} %constant_dynamic-update-slice_fusion, f32[2048,384]{1,0:T(8,128)S(1)} %maximum_multiply_fusion), kind=kOutput, calls=%fused_computation.21 | convolution fusion | flops 1811939328 | bytes 6881280 | tf_op jit(solution)/shard_map/dot_general | solution.py:221
  27.4 1.3 collective-permute-start.5
  28.7 17.1 %collective-permute-done.2 = f32[2048,128]{1,0:T(8,128)} collective-permute-done((f32[2048,128]{1,0:T(8,128)}, f32[2048,128]{1,0:T(8,128)}, u32[]{:S(2)}, u32[]{:S(2)}) %collective-permute-start.2) | collective-permute-done | bytes 1048608 | tf_op jit(solution)/shard_map/ppermute | solution.py:209
  45.8 0.0 collective-permute-done.3.across
  45.8 1.9 %broadcast_multiply_fusion = f32[2048,128]{1,0:T(8,128)S(1)} fusion(f32[2048,128]{1,0:T(8,128)} %collective-permute-done.2, f32[2048]{0:T(1024)S(1)} %copy-done.9), kind=kLoop, calls=%fused_computation.11 | loop fusion | flops 262144 | bytes 2105344 | tf_op jit(solution)/shard_map/mul | solution.py:223
  47.7 2.7 %fusion.11 = f32[384,128]{1,0:T(8,128)S(1)} fusion(f32[2048,384]{1,0:T(8,128)S(1)} %constant_dynamic-update-slice_fusion, f32[2048,128]{1,0:T(8,128)S(1)} %broadcast_multiply_fusion), kind=kOutput, calls=%fused_computation.22 | convolution fusion | flops 603979776 | bytes 4390912 | tf_op jit(solution)/shard_map/dot_general | solution.py:224
  50.4 1.6 fusion
  52.0 0.1 fusion.5
  52.1 7.1 %collective-permute-start.4 = (f32[512,256]{1,0:T(8,128)S(1)}, f32[512,256]{1,0:T(8,128)S(1)}, u32[]{:S(2)}, u32[]{:S(2)}) collective-permute-start(f32[512,256]{1,0:T(8,128)S(1)} %fusion.5), channel_id=1, source_target_pairs={{0,4},{4,0},{1,5},{5,1},{2,6},{6,2},{3,7},{7,3},{8,12},{12,8},{9,1... | collective-permute-start | bytes 1572872 | tf_op jit(solution)/shard_map/ppermute | solution.py:235
  59.3 1.5 collective-permute-done.4
  60.8 0.1 select_add_fusion
  60.9 0.0 collective-permute-done.5.outward
  60.9 0.0 copy-start.3
  60.9 1.0 copy-done.3
  61.9 26.8 %all_to_all.32 = f32[32,16,256]{2,1,0:T(8,128)} all-to-all(f32[32,16,256]{2,1,0:T(8,128)S(1)} %bitcast.16), channel_id=1, replica_groups=mesh['x'=4,'z'=8,'yh'=2,'core'=2,'state'=4] {'x','z'}, dimensions={0} | all-to-all | bytes 1048576 | tf_op jit(solution)/shard_map/all_to_all | solution.py:26
  88.6 1.1 reduce_sum.18
  89.7 18.0 %all_to_all.33 = f32[8,16,256]{2,1,0:T(8,128)S(1)} all-to-all(f32[8,16,256]{2,1,0:T(8,128)S(1)} %broadcast_in_dim.11), channel_id=1, replica_groups=mesh['x'=4,'z'=8,'yh'=2,'core'=2,'state'=4] {'yh','state'}, dimensions={0} | all-to-all | bytes 262144 | tf_op jit(solution)/shard_map/all_to_all | solution.py:26
  107.8 0.1 broadcast_in_dim.12
  107.8 20.4 %all_to_all.34 = f32[32,32,128]{2,1,0:T(8,128)} all-to-all(f32[32,32,128]{2,1,0:T(8,128)S(1)} %broadcast_in_dim.12), channel_id=1, replica_groups=mesh['x'=4,'z'=8,'yh'=2,'core'=2,'state'=4] {'x','z'}, dimensions={0} | all-to-all | bytes 1048576 | tf_op jit(solution)/shard_map/all_to_all | solution.py:26
  128.2 7.0 %collective-permute-start.6 = (f32[1024,128]{1,0:T(8,128)}, f32[1024,128]{1,0:T(8,128)}, u32[]{:S(2)}, u32[]{:S(2)}) collective-permute-start(f32[1024,128]{1,0:T(8,128)} %bitcast.9.own), channel_id=1, source_target_pairs={{0,4},{4,0},{1,5},{5,1},{2,6},{6,2},{3,7},{7,3},{8,12},{12,8},{9,1... | collective-permute-start | bytes 1572872 | tf_op jit(solution)/shard_map/ppermute | solution.py:243
  135.2 0.1 pad_add_fusion.place_ref
  135.3 1.3 collective-permute-start.7
  136.6 0.9 broadcast_in_dim.13
  137.5 5.6 %all-to-all-start.3 = ((f32[32,32,128]{2,1,0:T(8,128)}), f32[32,32,128]{2,1,0:T(8,128)}, u32[]{:S(2)}, u32[]{:S(2)}) async-start(f32[32,32,128]{2,1,0:T(8,128)} %broadcast_in_dim.13), calls=%async_computation.3 | async-start | bytes 1048576 | tf_op jit(solution)/shard_map/all_to_all | solution.py:26
  143.1 0.0 collective-permute-done.6.other
  143.1 0.0 copy-start.5
  143.1 0.9 copy-done.5
  144.1 21.8 %shard_map.59 = (f32[512,128]{1,0:T(8,128)S(1)}, f32[512,512]{1,0:T(8,128)S(1)}) custom-call(s32[2]{0:T(128)S(1)} %pad_add_fusion.place_ref, f32[1024,128]{1,0:T(8,128)} %bitcast.9.own, f32[1024,128]{1,0:T(8,128)} %collective-permute-done.6.other, f32[512,128]{1,0:T(8,128)S(1)} %copy-done.5), custom_call_target="tpu_custom_call" | custom-call | flops 20000000000 | bytes 4194304 | tf_op jit(solution)/shard_map/pallas_call | solution.py:135
  165.9 1.0 copy-done.6
  166.8 0.0 all-to-all-done.3
  166.8 2.2 %collective-permute-start.8 = (f32[1024,128]{1,0:T(8,128)}, f32[1024,128]{1,0:T(8,128)}, u32[]{:S(2)}, u32[]{:S(2)}) collective-permute-start(f32[1024,128]{1,0:T(8,128)} %bitcast.10.own), channel_id=1, source_target_pairs={{0,4},{4,0},{1,5},{5,1},{2,6},{6,2},{3,7},{7,3},{8,12},{12,8},{9,1... | collective-permute-start | bytes 1572872 | tf_op jit(solution)/shard_map/ppermute | solution.py:246
  169.1 0.1 stack.34.source_ref
  169.2 0.0 collective-permute-done.7.far
  169.2 1.2 copy-done.2
  170.4 1.2 copy-done.4
  171.6 4.3 %shard_map.60 = f32[2048,128]{1,0:T(8,128)} custom-call(s32[5]{0:T(128)S(1)} %stack.34.source_ref, f32[512,128]{1,0:T(8,128)S(1)} %get-tuple-element.12.rotation_ref, f32[2048,128]{1,0:T(8,128)S(1)} %copy-done, f32[2048,128]{1,0:T(8,128)S(1)} %collective-permute-done.pairs, f32[2048,128]{1,0:T(8,128)S(1)} %collective-permute-done.1.middle, ...), custom_call_target="tpu_custom_call" | custom-call | flops 2000000000 | bytes 8388608 | tf_op jit(solution)/shard_map/pallas_call | solution.py:187
  175.9 0.0 collective-permute-done.8.other
  176.0 4.5 %shard_map.61 = f32[512,128]{1,0:T(8,128)} custom-call(s32[2]{0:T(128)S(1)} %pad_add_fusion.place_ref, f32[1024,128]{1,0:T(8,128)} %bitcast.10.own, f32[1024,128]{1,0:T(8,128)} %collective-permute-done.8.other, f32[512,512]{1,0:T(8,128)S(1)} %copy-done.7), custom_call_target="tpu_custom_call" | custom-call | flops 1000000000 | bytes 4194304 | tf_op jit(solution)/shard_map/pallas_call | solution.py:135
  (22 shorter events, 0.1 us)
Async XLA Ops:
  0.6 22.7 %collective-permute-start = (f32[2048,128]{1,0:T(8,128)}, f32[2048,128]{1,0:T(8,128)S(1)}, u32[]{:S(2)}, u32[]{:S(2)}) collective-permute-start(f32[2048,128]{1,0:T(8,128)} %own.1), channel_id=1, source_target_pairs={{0,1},{1,0},{2,3},{3,2},{4,5},{5,4},{6,7},{7,6},{8,9},{9,8},{10,11... | collective-permute-start | bytes 3145736 | tf_op jit(solution)/shard_map/ppermute | solution.py:207
  4.7 19.4 %collective-permute-start.1 = (f32[2048,128]{1,0:T(8,128)}, f32[2048,128]{1,0:T(8,128)S(1)}, u32[]{:S(2)}, u32[]{:S(2)}) collective-permute-start(f32[2048,128]{1,0:T(8,128)} %own.1), channel_id=1, source_target_pairs={{1,2},{2,1},{5,6},{6,5},{9,10},{10,9},{13,14},{14,13},{17,18},{18,... | collective-permute-start | bytes 3145736 | tf_op jit(solution)/shard_map/ppermute | solution.py:208
  5.4 40.3 %collective-permute-start.2 = (f32[2048,128]{1,0:T(8,128)}, f32[2048,128]{1,0:T(8,128)}, u32[]{:S(2)}, u32[]{:S(2)}) collective-permute-start(f32[2048,128]{1,0:T(8,128)} %param.5), channel_id=1, source_target_pairs={{0,1},{3,2},{4,5},{7,6},{8,9},{11,10},{12,13},{15,14},{16,17},{19,... | collective-permute-start | bytes 3145736 | tf_op jit(solution)/shard_map/ppermute | solution.py:209
  12.1 12.1 %copy-start = (f32[2048,128]{1,0:T(8,128)S(1)}, f32[2048,128]{1,0:T(8,128)}, u32[]{:S(2)}) copy-start(f32[2048,128]{1,0:T(8,128)} %own.1) | copy-start | bytes 3145732
  12.1 12.1 %copy-start.8 = (f32[2048,128]{1,0:T(8,128)S(1)}, f32[2048,128]{1,0:T(8,128)}, u32[]{:S(2)}) copy-start(f32[2048,128]{1,0:T(8,128)} %param.5) | copy-start | bytes 3145732
  12.1 12.1 %copy-start.9 = (f32[2048]{0:T(1024)S(1)}, f32[2048]{0:T(1024)}, u32[]{:S(2)}) copy-start(f32[2048]{0:T(1024)} %param.6) | copy-start | bytes 24580
  23.3 22.5 %collective-permute-start.3 = (f32[2048,128]{1,0:T(8,128)S(1)}, f32[2048,128]{1,0:T(8,128)S(1)}, u32[]{:S(2)}, u32[]{:S(2)}) collective-permute-start(f32[2048,128]{1,0:T(8,128)S(1)} %collective-permute-done.pairs), channel_id=1, source_target_pairs={{1,2},{2,1},{5,6},{6,5},{9,10},{10,9},{13,14},{14,13},{17,18},{18,... | collective-permute-start | bytes 3145736 | tf_op jit(solution)/shard_map/ppermute | solution.py:210
  27.4 33.5 %collective-permute-start.5 = (f32[2048,128]{1,0:T(8,128)S(1)}, f32[2048,128]{1,0:T(8,128)S(1)}, u32[]{:S(2)}, u32[]{:S(2)}) collective-permute-start(f32[2048,128]{1,0:T(8,128)S(1)} %collective-permute-done.1.middle), channel_id=1, source_target_pairs={{1,0},{2,3},{5,4},{6,7},{9,8},{10,11},{13,12},{14,15},{17,16},{18,... | collective-permute-start | bytes 3145736 | tf_op jit(solution)/shard_map/ppermute | solution.py:211
  45.8 4.6 %copy-start.1 = (f32[2048,128]{1,0:T(8,128)}, f32[2048,128]{1,0:T(8,128)S(1)}, u32[]{:S(2)}) copy-start(f32[2048,128]{1,0:T(8,128)S(1)} %collective-permute-done.3.across) | copy-start | bytes 3145732
  52.1 8.7 %collective-permute-start.4 = (f32[512,256]{1,0:T(8,128)S(1)}, f32[512,256]{1,0:T(8,128)S(1)}, u32[]{:S(2)}, u32[]{:S(2)}) collective-permute-start(f32[512,256]{1,0:T(8,128)S(1)} %fusion.5), channel_id=1, source_target_pairs={{0,4},{4,0},{1,5},{5,1},{2,6},{6,2},{3,7},{7,3},{8,12},{12,8},{9,1... | collective-permute-start | bytes 1572872 | tf_op jit(solution)/shard_map/ppermute | solution.py:235
  60.9 1.0 copy-start.3
  128.2 14.9 %collective-permute-start.6 = (f32[1024,128]{1,0:T(8,128)}, f32[1024,128]{1,0:T(8,128)}, u32[]{:S(2)}, u32[]{:S(2)}) collective-permute-start(f32[1024,128]{1,0:T(8,128)} %bitcast.9.own), channel_id=1, source_target_pairs={{0,4},{4,0},{1,5},{5,1},{2,6},{6,2},{3,7},{7,3},{8,12},{12,8},{9,1... | collective-permute-start | bytes 1572872 | tf_op jit(solution)/shard_map/ppermute | solution.py:243
  135.3 33.8 %collective-permute-start.7 = (f32[2048,128]{1,0:T(8,128)}, f32[2048,128]{1,0:T(8,128)}, u32[]{:S(2)}, u32[]{:S(2)}) collective-permute-start(f32[2048,128]{1,0:T(8,128)} %copy-done.1), channel_id=1, source_target_pairs={{1,0},{2,3},{5,4},{6,7},{9,8},{10,11},{13,12},{14,15},{17,16},{18,... | collective-permute-start | bytes 3145736 | tf_op jit(solution)/shard_map/ppermute | solution.py:212
  137.5 29.4 %all-to-all-start.3 = ((f32[32,32,128]{2,1,0:T(8,128)}), f32[32,32,128]{2,1,0:T(8,128)}, u32[]{:S(2)}, u32[]{:S(2)}) async-start(f32[32,32,128]{2,1,0:T(8,128)} %broadcast_in_dim.13), calls=%async_computation.3 | async-start | bytes 1048576 | tf_op jit(solution)/shard_map/all_to_all | solution.py:26
  143.1 1.0 copy-start.5
  165.9 1.0 copy-start.6
  166.8 9.1 %collective-permute-start.8 = (f32[1024,128]{1,0:T(8,128)}, f32[1024,128]{1,0:T(8,128)}, u32[]{:S(2)}, u32[]{:S(2)}) collective-permute-start(f32[1024,128]{1,0:T(8,128)} %bitcast.10.own), channel_id=1, source_target_pairs={{0,4},{4,0},{1,5},{5,1},{2,6},{6,2},{3,7},{7,3},{8,12},{12,8},{9,1... | collective-permute-start | bytes 1572872 | tf_op jit(solution)/shard_map/ppermute | solution.py:246
  169.2 1.2 copy-start.2
  170.4 1.2 copy-start.4
  171.6 4.3 %copy-start.7 = (f32[512,512]{1,0:T(8,128)S(1)}, f32[512,512]{1,0:T(8,128)}, u32[]{:S(2)}) copy-start(f32[512,512]{1,0:T(8,128)} %copy-done.6) | copy-start | bytes 3145732

commit v6 on v3

--- a/solution.py
+++ b/solution.py
@@ -69,6 +69,17 @@
     return right
 
 
+def high_low(value):
+    high = value.astype(jnp.bfloat16)
+    return high, (value - high.astype(jnp.float32)).astype(jnp.bfloat16)
+
+
+def three_products(left, right, numbers):
+    (left_high, left_low), (right_high, right_low) = high_low(left), high_low(right)
+    times = functools.partial(lax.dot_general, dimension_numbers=numbers, preferred_element_type=jnp.float32)
+    return times(left_high, right_high) + (times(left_high, right_low) + times(left_low, right_high))
+
+
 def unpack(packed, matrix):
     panels = matrix.shape[1] // EDGE
     for run in range(matrix.shape[0] // RUN):
@@ -121,10 +132,10 @@
         low, high = EDGE * j, EDGE * (j + 1)
         rotation_ref[low:high, :] = dot(inverse[low:, low:high], coefficients[low:, :], BY_COLS)
     own = pl.ds(pl.multiple_of(place_ref[1] * EDGE, EDGE), EDGE)
-    half = dot(hamil[...], inverse[own, :], BY_ROWS)
+    half = three_products(hamil[...], inverse[own, :], BY_ROWS)
     for j in range(blocks):
         high = EDGE * (j + 1)
-        projected_ref[high - EDGE : high, :] = dot(inverse[high - EDGE : high, :high], half[:high], PLAIN)
+        projected_ref[high - EDGE : high, :] = three_products(inverse[high - EDGE : high, :high], half[:high], PLAIN)
 
 
 def solve(place, own_packed, other_packed, coefficients):
@@ -141,11 +152,6 @@
         cost_estimate=pl.CostEstimate(flops=2 * 10**10, bytes_accessed=2**22, transcendentals=0),
         compiler_params=pltpu.CompilerParams(vmem_limit_bytes=32 * 2**20),
     )(place, own_packed, other_packed, coefficients)
-
-
-def high_low(value):
-    high = value.astype(jnp.bfloat16)
-    return high, (value - high.astype(jnp.float32)).astype(jnp.bfloat16)
 
 
 def rotate_rows(source_ref, rotation_ref, own, pairs, middle, outward, across, far, rotated_ref):
@@ -211,7 +217,6 @@
     kept, sent = jnp.where(core == 0, gram, hamil), jnp.where(core == 0, hamil, gram)
     summed = kept + lax.ppermute(sent, "core", [(0, 1), (1, 0)])
     summed = total(exchange(after(summed, outward), PLANE), PLANE)
-    summed = after(summed, far)
     shape = (lax.axis_size("yh"), lax.axis_size("state")) + summed.shape
     summed = jnp.sum(exchange(copies(summed, LINE), LINE).reshape(shape), axis=0)
     panels = summed[1][:, :width], summed[1][:, width:], summed[2][:, width:], summed[2][:, :width]

time: 179 us -> 177 us (0.989)
  blocking collectives: 74.9 us -> 72.8 us
    all_to_all x3, blocking collectives: 74.9 us -> 72.8 us  [exchange(): return lax.all_to_all(value, axes, 0, 0, tiled=True)]
  transfers between devices with their start and end apart: 8 -> 8, of which waited for: 4 -> 5; matrix products, arithmetic and copies ran while one was open for 5% -> 5% of each run, Pallas kernels for 0% -> 13%
where the time goes in v6:
time: 177 us
  blocking collectives  72.8 us (41%)
  waiting for transfers between devices  33.7 us (19%)
  starting transfers between devices  31.1 us (18%)
  Pallas kernels  28.1 us (16%)
  matrix products  8.75 us (5%)
    all_to_all x3, blocking collectives, exchange(): return lax.all_to_all(value, axes, 0, 0, tiled=True)  72.8 us
    pallas_call x1, Pallas kernels, solve(): pl.pallas_call(small_matrices, out_shape=(result, result), in_specs=[pl.B...  23.9 us
    ppermute x1, waiting for transfers between devices, shards(): outer_h = send(h_block, perm=[(0, 1), (3, 2)])  19.3 us
    ppermute x1, waiting for transfers between devices, shards(): pairs = send(x_block, perm=[(0, 1), (1, 0), (2, 3), (3, 2)])  11.2 us
    ppermute x1, starting transfers between devices, shards(): other = lax.ppermute(summed, 'core', [(0, 1), (1, 0)])  7.87 us
    ppermute x1, starting transfers between devices, shards(): summed = kept + lax.ppermute(sent, 'core', [(0, 1), (1, 0)])  7.14 us
    ppermute x1, starting transfers between devices, shards(): outer_h = send(h_block, perm=[(0, 1), (3, 2)])  6.69 us
    dot_general x1, matrix products, shards(): times(near, weighted)  5.63 us
  transfers between devices with their start and end apart: 8, of which 5 were waited for; matrix products, arithmetic and copies ran while one was open for 5% of the time, Pallas kernels for 13%

profile of v6, /device:TPU:1, one launch (start us, length us, event | category | flops | bytes accessed | tf_op | source)
XLA Modules:
  0.0 176.9 jit_solution(5802043724568774538)
XLA Ops:
  0.6 4.0 %collective-permute-start = (f32[2048,128]{1,0:T(8,128)}, f32[2048,128]{1,0:T(8,128)S(1)}, u32[]{:S(2)}, u32[]{:S(2)}) collective-permute-start(f32[2048,128]{1,0:T(8,128)} %own.1), channel_id=1, source_target_pairs={{0,1},{1,0},{2,3},{3,2},{4,5},{5,4},{6,7},{7,6},{8,9},{9,8},{10,11... | collective-permute-start | bytes 3145736 | tf_op jit(solution)/shard_map/ppermute | solution.py:200
  4.7 0.7 collective-permute-start.1
  5.4 6.7 %collective-permute-start.2 = (f32[2048,128]{1,0:T(8,128)}, f32[2048,128]{1,0:T(8,128)}, u32[]{:S(2)}, u32[]{:S(2)}) collective-permute-start(f32[2048,128]{1,0:T(8,128)} %param.5), channel_id=1, source_target_pairs={{0,1},{3,2},{4,5},{7,6},{8,9},{11,10},{12,13},{15,14},{16,17},{19,... | collective-permute-start | bytes 3145736 | tf_op jit(solution)/shard_map/ppermute | solution.py:202
  12.1 11.2 %collective-permute-done.pairs = f32[2048,128]{1,0:T(8,128)S(1)} collective-permute-done((f32[2048,128]{1,0:T(8,128)}, f32[2048,128]{1,0:T(8,128)S(1)}, u32[]{:S(2)}, u32[]{:S(2)}) %collective-permute-start) | collective-permute-done | bytes 1048608 | tf_op jit(solution)/shard_map/ppermute | solution.py:200
  23.3 1.6 collective-permute-start.3
  24.9 0.0 copy-start
  24.9 0.0 copy-start.6
  24.9 0.0 copy-start.7
  24.9 0.0 collective-permute-done.1.middle
  24.9 0.0 copy-start.1
  24.9 1.6 collective-permute-start.5
  26.5 19.3 %collective-permute-done.2 = f32[2048,128]{1,0:T(8,128)} collective-permute-done((f32[2048,128]{1,0:T(8,128)}, f32[2048,128]{1,0:T(8,128)}, u32[]{:S(2)}, u32[]{:S(2)}) %collective-permute-start.2) | collective-permute-done | bytes 1048608 | tf_op jit(solution)/shard_map/ppermute | solution.py:202
  45.8 5.6 %fusion = f32[384,512]{1,0:T(8,128)S(1)} fusion(f32[2048,128]{1,0:T(8,128)S(1)} %collective-permute-done.1.middle, f32[2048,128]{1,0:T(8,128)S(1)} %collective-permute-done.pairs, f32[2048,128]{1,0:T(8,128)} %own.1, f32[2048,128]{1,0:T(8,128)} %param.5, f32[2048,128]{1,0:T(8,128)} %collective-permute-done.2, f32[2048]{0:T(1024)} %param.6), kind=kOutput, calls=%fused_computation.1 | convolution fusion | flops 2421686272 | bytes 6037504 | tf_op jit(solution)/shard_map/dot_general | solution.py:214
  51.4 0.0 copy-done.1
  51.4 0.0 collective-permute-done.3.across
  51.4 0.0 copy-done
  51.4 0.0 copy-done.6
  51.4 0.0 copy-done.7
  51.4 3.1 %fusion.9 = f32[128,512]{1,0:T(8,128)S(1)} fusion(f32[2048,128]{1,0:T(8,128)} %collective-permute-done.3.across, f32[2048,128]{1,0:T(8,128)S(1)} %copy-done.6, f32[2048,128]{1,0:T(8,128)} %collective-permute-done.2, f32[2048,128]{1,0:T(8,128)S(1)} %copy-done, f32[2048,128]{1,0:T(8,128)S(1)} %collective-permute-done.pairs, f32[2048]{0:T(1024)S(1)} %copy-done.7), kind=kOutput, calls=%fused_computation.10 | convolution fusion | flops 809500672 | bytes 5513216 | tf_op jit(solution)/shard_map/dot_general | solution.py:214
  54.6 0.1 broadcast_select_fusion
  54.6 7.1 %collective-permute-start.4 = (f32[512,256]{1,0:T(8,128)S(1)}, f32[512,256]{1,0:T(8,128)S(1)}, u32[]{:S(2)}, u32[]{:S(2)}) collective-permute-start(f32[512,256]{1,0:T(8,128)S(1)} %broadcast_select_fusion), channel_id=1, source_target_pairs={{0,4},{4,0},{1,5},{5,1},{2,6},{6,2},{3,7},{7,3},{8,12},{12,8},{9,1... | collective-permute-start | bytes 1572872 | tf_op jit(solution)/shard_map/ppermute | solution.py:218
  61.8 1.5 collective-permute-done.4
  63.3 0.1 select_add_fusion
  63.5 0.0 collective-permute-done.5.outward
  63.5 0.0 copy-start.3
  63.5 1.0 copy-done.3
  64.5 26.6 %all_to_all.23 = f32[32,16,256]{2,1,0:T(8,128)S(1)} all-to-all(f32[32,16,256]{2,1,0:T(8,128)S(1)} %bitcast.18), channel_id=1, replica_groups=mesh['x'=4,'z'=8,'yh'=2,'core'=2,'state'=4] {'x','z'}, dimensions={0} | all-to-all | bytes 1048576 | tf_op jit(solution)/shard_map/all_to_all | solution.py:26
  91.2 14.7 %all_to_all.24 = f32[8,16,256]{2,1,0:T(8,128)S(1)} all-to-all(f32[8,16,256]{2,1,0:T(8,128)S(1)} %broadcast_in_dim.7), channel_id=1, replica_groups=mesh['x'=4,'z'=8,'yh'=2,'core'=2,'state'=4] {'yh','state'}, dimensions={0} | all-to-all | bytes 262144 | tf_op jit(solution)/shard_map/all_to_all | solution.py:26
  105.9 0.1 broadcast_in_dim.8
  106.0 0.0 copy-start.5
  106.0 31.5 %all_to_all.25 = f32[32,64,128]{2,1,0:T(8,128)S(1)} all-to-all(f32[32,64,128]{2,1,0:T(8,128)S(1)} %broadcast_in_dim.8), channel_id=1, replica_groups=mesh['x'=4,'z'=8,'yh'=2,'core'=2,'state'=4] {'x','z'}, dimensions={0} | all-to-all | bytes 2097152 | tf_op jit(solution)/shard_map/all_to_all | solution.py:26
  137.5 7.9 %collective-permute-start.6 = (f32[2048,128]{1,0:T(8,128)S(1)}, f32[2048,128]{1,0:T(8,128)}, u32[]{:S(2)}, u32[]{:S(2)}) collective-permute-start(f32[2048,128]{1,0:T(8,128)S(1)} %bitcast.16), channel_id=1, source_target_pairs={{0,4},{4,0},{1,5},{5,1},{2,6},{6,2},{3,7},{7,3},{8,12},{12,8},{9,1... | collective-permute-start | bytes 3145736 | tf_op jit(solution)/shard_map/ppermute | solution.py:224
  145.4 0.1 stack.34.source_ref
  145.5 0.1 pad_add_fusion.place_ref
  145.6 0.0 copy-start.2
  145.6 0.0 copy-start.4
  145.6 1.4 collective-permute-start.7
  147.0 0.8 collective-permute-done.6.other_packed
  147.8 0.0 copy-done.5
  147.8 23.9 %shard_map.59 = (f32[512,128]{1,0:T(8,128)S(1)}, f32[512,128]{1,0:T(8,128)}) custom-call(s32[2]{0:T(128)S(1)} %pad_add_fusion.place_ref, f32[2048,128]{1,0:T(8,128)S(1)} %bitcast.17, f32[2048,128]{1,0:T(8,128)} %collective-permute-done.6.other_packed, f32[512,128]{1,0:T(8,128)S(1)} %copy-done.5), custom_call_target="tpu_custom_call" | custom-call | flops 20000000000 | bytes 4194304 | tf_op jit(solution)/shard_map/pallas_call | solution.py:146
  171.7 0.9 collective-permute-done.7.far
  172.6 0.0 copy-done.2
  172.6 0.0 copy-done.4
  172.6 4.2 %shard_map.60 = f32[2048,128]{1,0:T(8,128)} custom-call(s32[5]{0:T(128)S(1)} %stack.34.source_ref, f32[512,128]{1,0:T(8,128)S(1)} %get-tuple-element.6.rotation_ref, f32[2048,128]{1,0:T(8,128)S(1)} %copy-done, f32[2048,128]{1,0:T(8,128)S(1)} %collective-permute-done.pairs, f32[2048,128]{1,0:T(8,128)S(1)} %copy-done.2, f32[2048,128]{1,0:T(8,128)S(1)} %copy-done.4, ...), custom_call_target="tpu_custom_call" | custom-call | flops 2000000000 | bytes 8388608 | tf_op jit(solution)/shard_map/pallas_call | solution.py:180
  (6 shorter events, 0.1 us)
Async XLA Ops:
  0.6 22.7 %collective-permute-start = (f32[2048,128]{1,0:T(8,128)}, f32[2048,128]{1,0:T(8,128)S(1)}, u32[]{:S(2)}, u32[]{:S(2)}) collective-permute-start(f32[2048,128]{1,0:T(8,128)} %own.1), channel_id=1, source_target_pairs={{0,1},{1,0},{2,3},{3,2},{4,5},{5,4},{6,7},{7,6},{8,9},{9,8},{10,11... | collective-permute-start | bytes 3145736 | tf_op jit(solution)/shard_map/ppermute | solution.py:200
  4.7 20.2 %collective-permute-start.1 = (f32[2048,128]{1,0:T(8,128)}, f32[2048,128]{1,0:T(8,128)S(1)}, u32[]{:S(2)}, u32[]{:S(2)}) collective-permute-start(f32[2048,128]{1,0:T(8,128)} %own.1), channel_id=1, source_target_pairs={{1,2},{2,1},{5,6},{6,5},{9,10},{10,9},{13,14},{14,13},{17,18},{18,... | collective-permute-start | bytes 3145736 | tf_op jit(solution)/shard_map/ppermute | solution.py:201
  5.4 40.3 %collective-permute-start.2 = (f32[2048,128]{1,0:T(8,128)}, f32[2048,128]{1,0:T(8,128)}, u32[]{:S(2)}, u32[]{:S(2)}) collective-permute-start(f32[2048,128]{1,0:T(8,128)} %param.5), channel_id=1, source_target_pairs={{0,1},{3,2},{4,5},{7,6},{8,9},{11,10},{12,13},{15,14},{16,17},{19,... | collective-permute-start | bytes 3145736 | tf_op jit(solution)/shard_map/ppermute | solution.py:202
  23.3 28.1 %collective-permute-start.3 = (f32[2048,128]{1,0:T(8,128)S(1)}, f32[2048,128]{1,0:T(8,128)}, u32[]{:S(2)}, u32[]{:S(2)}) collective-permute-start(f32[2048,128]{1,0:T(8,128)S(1)} %collective-permute-done.pairs), channel_id=1, source_target_pairs={{1,2},{2,1},{5,6},{6,5},{9,10},{10,9},{13,14},{14,13},{17,18},{18,... | collective-permute-start | bytes 3145736 | tf_op jit(solution)/shard_map/ppermute | solution.py:203
  24.9 26.5 %copy-start = (f32[2048,128]{1,0:T(8,128)S(1)}, f32[2048,128]{1,0:T(8,128)}, u32[]{:S(2)}) copy-start(f32[2048,128]{1,0:T(8,128)} %own.1) | copy-start | bytes 3145732
  24.9 26.5 %copy-start.6 = (f32[2048,128]{1,0:T(8,128)S(1)}, f32[2048,128]{1,0:T(8,128)}, u32[]{:S(2)}) copy-start(f32[2048,128]{1,0:T(8,128)} %param.5) | copy-start | bytes 3145732
  24.9 26.5 %copy-start.7 = (f32[2048]{0:T(1024)S(1)}, f32[2048]{0:T(1024)}, u32[]{:S(2)}) copy-start(f32[2048]{0:T(1024)} %param.6) | copy-start | bytes 24580
  24.9 26.5 %copy-start.1 = (f32[2048,128]{1,0:T(8,128)}, f32[2048,128]{1,0:T(8,128)S(1)}, u32[]{:S(2)}) copy-start(f32[2048,128]{1,0:T(8,128)S(1)} %collective-permute-done.1.middle) | copy-start | bytes 3145732
  24.9 38.5 %collective-permute-start.5 = (f32[2048,128]{1,0:T(8,128)S(1)}, f32[2048,128]{1,0:T(8,128)S(1)}, u32[]{:S(2)}, u32[]{:S(2)}) collective-permute-start(f32[2048,128]{1,0:T(8,128)S(1)} %collective-permute-done.1.middle), channel_id=1, source_target_pairs={{1,0},{2,3},{5,4},{6,7},{9,8},{10,11},{13,12},{14,15},{17,16},{18,... | collective-permute-start | bytes 3145736 | tf_op jit(solution)/shard_map/ppermute | solution.py:204
  54.6 8.7 %collective-permute-start.4 = (f32[512,256]{1,0:T(8,128)S(1)}, f32[512,256]{1,0:T(8,128)S(1)}, u32[]{:S(2)}, u32[]{:S(2)}) collective-permute-start(f32[512,256]{1,0:T(8,128)S(1)} %broadcast_select_fusion), channel_id=1, source_target_pairs={{0,4},{4,0},{1,5},{5,1},{2,6},{6,2},{3,7},{7,3},{8,12},{12,8},{9,1... | collective-permute-start | bytes 1572872 | tf_op jit(solution)/shard_map/ppermute | solution.py:218
  63.5 1.0 copy-start.3
  106.0 41.8 %copy-start.5 = (f32[512,128]{1,0:T(8,128)S(1)}, f32[512,128]{1,0:T(8,128)}, u32[]{:S(2)}) copy-start(f32[512,128]{1,0:T(8,128)} %coefficients.1) | copy-start | bytes 786436
  137.5 10.3 %collective-permute-start.6 = (f32[2048,128]{1,0:T(8,128)S(1)}, f32[2048,128]{1,0:T(8,128)}, u32[]{:S(2)}, u32[]{:S(2)}) collective-permute-start(f32[2048,128]{1,0:T(8,128)S(1)} %bitcast.16), channel_id=1, source_target_pairs={{0,4},{4,0},{1,5},{5,1},{2,6},{6,2},{3,7},{7,3},{8,12},{12,8},{9,1... | collective-permute-start | bytes 3145736 | tf_op jit(solution)/shard_map/ppermute | solution.py:224
  145.6 27.0 %copy-start.2 = (f32[2048,128]{1,0:T(8,128)S(1)}, f32[2048,128]{1,0:T(8,128)}, u32[]{:S(2)}) copy-start(f32[2048,128]{1,0:T(8,128)} %copy-done.1) | copy-start | bytes 3145732
  145.6 27.0 %copy-start.4 = (f32[2048,128]{1,0:T(8,128)S(1)}, f32[2048,128]{1,0:T(8,128)}, u32[]{:S(2)}) copy-start(f32[2048,128]{1,0:T(8,128)} %copy-done.3) | copy-start | bytes 3145732
  145.6 27.0 %collective-permute-start.7 = (f32[2048,128]{1,0:T(8,128)}, f32[2048,128]{1,0:T(8,128)S(1)}, u32[]{:S(2)}, u32[]{:S(2)}) collective-permute-start(f32[2048,128]{1,0:T(8,128)} %collective-permute-done.3.across), channel_id=1, source_target_pairs={{1,0},{2,3},{5,4},{6,7},{9,8},{10,11},{13,12},{14,15},{17,16},{18,... | collective-permute-start | bytes 3145736 | tf_op jit(solution)/shard_map/ppermute | solution.py:205
